TPU v7x, 256 devices: a whole 4x4x8 slice. The times are simulated.
256 devices in a mesh: gx: 16 (over z_hi, x), gy: 16 (over z_lo, y, core).
Axes of the slice: x: 4, y: 4, z: 8 (z_hi: 4, z_lo: 2; z = z_hi * 2 + z_lo), core: 2. Of those that a mesh axis runs over, the one named last changes fastest.
Arguments:
- fields: float32 [6, 48, 128, 2048], P(None, None, 'gx', 'gy'), may hold values from -6 to 6
- adjoint: float32 [6, 48, 128, 2048], P(None, None, 'gx', 'gy'), may hold values from -6 to 6
- permittivity: float32 [48, 128, 2048], P(None, 'gx', 'gy'), may hold values from 1 to 12
- lists: int32 [256, 128], replicated, may hold values from 0 to 255, all different within a row
- mask: int32 [256], replicated, may hold values 0 or 1
Outputs:
- fields_next: float32 [6, 48, 128, 2048], P(None, None, 'gx', 'gy')
- adjoint_next: float32 [6, 48, 128, 2048], P(None, None, 'gx', 'gy')
- sensitivity: float32 [48, 128, 2048], P(None, 'gx', 'gy')
- farfield: float32 [256, 8, 256], P(('gx', 'gy'))
Inputs may be any that keep to these rules, and one draw needn't show every extreme that they name: `lists`: each row names 128 different direction blocks, and every block is named by some row.
All inputs are finite; a program needn't handle non-finite values.
Results may differ from a plain program's by a relative error of at most 0.0003.
Values sent between devices are 32-bit elements; how exact they have to be, the bound alone decides.
A program may use at most 64 MiB of HBM per device.

v0:
```python
import math

import jax
import jax.numpy as jnp
from jax import lax
from jax.sharding import PartitionSpec as P

DIRS_U = 256
DIRS_V = 256
ZM = 36


TIME_STEP = 0.5
PHASE_STEP = 0.3
OMEGA = PHASE_STEP / TIME_STEP
HIGHEST = lax.Precision.HIGHEST


def shifted(value, axis, steps):
    count = lax.axis_size(axis)
    initial, last = (max(0, -steps), min(count, count - steps))
    return lax.ppermute(value, axis, [(source, source + steps) for source in range(initial, last)])


def ahead(field, axis):
    length = field.shape[axis]
    rest = lax.slice_in_dim(field, 1, length, axis=axis)
    edge = jnp.zeros_like(lax.slice_in_dim(field, 0, 1, axis=axis))
    return jnp.concatenate([rest, edge], axis=axis) - field


def behind(field, axis):
    length = field.shape[axis]
    rest = lax.slice_in_dim(field, 0, length - 1, axis=axis)
    edge = jnp.zeros_like(lax.slice_in_dim(field, 0, 1, axis=axis))
    return field - jnp.concatenate([edge, rest], axis=axis)


def next_along(field, border, axis):
    length = field.shape[axis]
    rest = lax.slice_in_dim(field, 1, length, axis=axis)
    return jnp.concatenate([rest, jnp.expand_dims(border, axis)], axis=axis)


def previous_along(field, border, axis):
    length = field.shape[axis]
    rest = lax.slice_in_dim(field, 0, length - 1, axis=axis)
    return jnp.concatenate([jnp.expand_dims(border, axis), rest], axis=axis)


def leap_magnetic(state):
    electric = state[:, 0:3]
    border_x = shifted(electric[:, 1:3, :, 0, :], "gx", -1)
    border_y = shifted(electric[:, 0:3:2, :, :, 0], "gy", -1)
    electric_x, electric_y, electric_z = (state[:, 0], state[:, 1], state[:, 2])
    ahead_yz = next_along(electric_z, border_y[:, 1], 3) - electric_z
    ahead_xz = next_along(electric_z, border_x[:, 1], 2) - electric_z
    ahead_xy = next_along(electric_y, border_x[:, 0], 2) - electric_y
    ahead_yx = next_along(electric_x, border_y[:, 0], 3) - electric_x
    magnetic_x = state[:, 3] - TIME_STEP * (ahead_yz - ahead(electric_y, 1))
    magnetic_y = state[:, 4] - TIME_STEP * (ahead(electric_x, 1) - ahead_xz)
    magnetic_z = state[:, 5] - TIME_STEP * (ahead_xy - ahead_yx)
    return jnp.stack(
        [electric_x, electric_y, electric_z, magnetic_x, magnetic_y, magnetic_z], axis=1
    )


def leap_electric(state, update_scale):
    magnetic = state[:, 3:6]
    border_x = shifted(magnetic[:, 1:3, :, -1, :], "gx", 1)
    border_y = shifted(magnetic[:, 0:3:2, :, :, -1], "gy", 1)
    magnetic_x, magnetic_y, magnetic_z = (state[:, 3], state[:, 4], state[:, 5])
    behind_yz = magnetic_z - previous_along(magnetic_z, border_y[:, 1], 3)
    behind_xz = magnetic_z - previous_along(magnetic_z, border_x[:, 1], 2)
    behind_xy = magnetic_y - previous_along(magnetic_y, border_x[:, 0], 2)
    behind_yx = magnetic_x - previous_along(magnetic_x, border_y[:, 0], 3)
    electric_x = state[:, 0] + update_scale * (behind_yz - behind(magnetic_y, 1))
    electric_y = state[:, 1] + update_scale * (behind(magnetic_x, 1) - behind_xz)
    electric_z = state[:, 2] + update_scale * (behind_xy - behind_yx)
    return jnp.stack(
        [electric_x, electric_y, electric_z, magnetic_x, magnetic_y, magnetic_z], axis=1
    )


def weights_at(moment):
    theta = PHASE_STEP * moment
    return (math.cos(theta) * TIME_STEP, -math.sin(theta) * TIME_STEP)


def sweep(state, update_scale):
    count = state.shape[0]
    shape = state.shape[2:]
    spectrum_real = jnp.zeros((count, 3) + shape, jnp.float32)
    spectrum_imag = jnp.zeros((count, 3) + shape, jnp.float32)
    plane_real = jnp.zeros((count, 2) + shape[1:], jnp.float32)
    plane_imag = jnp.zeros((count, 2) + shape[1:], jnp.float32)
    for step in (1, 2):
        state = leap_magnetic(state)
        weight_real, weight_imag = weights_at(step - 0.5)
        monitor_h = state[:, 3:5, ZM]
        plane_real = plane_real + weight_real * monitor_h
        plane_imag = plane_imag + weight_imag * monitor_h
        state = leap_electric(state, update_scale)
        weight_real, weight_imag = weights_at(step)
        spectrum_real = spectrum_real + weight_real * state[:, 0:3]
        spectrum_imag = spectrum_imag + weight_imag * state[:, 0:3]
    return (state, spectrum_real, spectrum_imag, plane_real, plane_imag)


def monitor(spectrum_real, spectrum_imag, plane_real, plane_imag):
    electric_real = spectrum_real[:, ZM]
    electric_imag = spectrum_imag[:, ZM]
    return jnp.stack(
        [
            -plane_real[1],
            plane_real[0],
            electric_real[1],
            -electric_real[0],
            -plane_imag[1],
            plane_imag[0],
            electric_imag[1],
            -electric_imag[0],
        ]
    )


def phase_table(index, coords, count):
    slope = (2 * index + 1 - count)[:, None]
    turns = slope * coords[..., None, :] % (16 * count)
    angle = turns.astype(jnp.float32) * (2.0 * math.pi / (16 * count))
    return (jnp.cos(angle), jnp.sin(angle))


def rotate_rows(cosine, sine, real, imag):
    first = jnp.einsum("ux,cxy->cuy", cosine, real, precision=HIGHEST) + jnp.einsum(
        "ux,cxy->cuy", sine, imag, precision=HIGHEST
    )
    second = jnp.einsum("ux,cxy->cuy", cosine, imag, precision=HIGHEST) - jnp.einsum(
        "ux,cxy->cuy", sine, real, precision=HIGHEST
    )
    return (first, second)


def rotate_columns(real, imag, cosine, sine):
    first = jnp.einsum("cuy,vy->ucv", real, cosine, precision=HIGHEST) + jnp.einsum(
        "cuy,vy->ucv", imag, sine, precision=HIGHEST
    )
    second = jnp.einsum("cuy,vy->ucv", imag, cosine, precision=HIGHEST) - jnp.einsum(
        "cuy,vy->ucv", real, sine, precision=HIGHEST
    )
    return jnp.concatenate([first, second], axis=1)


def far_field(plane, lists, mask):
    width_x = plane.shape[1]
    width_y = plane.shape[2]
    scale = 1.0 / math.sqrt(width_x * width_y)
    count_x = lax.axis_size("gx")
    count_y = lax.axis_size("gy")
    tiles = count_x * count_y
    block_rows = DIRS_U // tiles
    index_x = lax.axis_index("gx")
    index_y = lax.axis_index("gy")
    own_tile = index_x * count_y + index_y
    tile_list = lax.dynamic_slice_in_dim(lists, own_tile, 1, 0)[0]
    weight = lax.dynamic_slice_in_dim(mask, own_tile, 1, 0)[0].astype(jnp.float32)
    coords_x = index_x * width_x + jnp.arange(width_x, dtype=jnp.int32)
    coords_y = index_y * width_y + jnp.arange(width_y, dtype=jnp.int32)
    cosine_v, sine_v = phase_table(jnp.arange(DIRS_V, dtype=jnp.int32), coords_y, DIRS_V)
    directions = jnp.arange(block_rows * lax.axis_size(("gx", "gy")), dtype=jnp.int32)
    cosine, sine = phase_table(directions, coords_x, DIRS_U)
    hits = (
        jnp.sum(
            (tile_list[None, :] == (directions // block_rows)[:, None]).astype(jnp.float32), axis=1
        )
        * weight
    )
    part_real, part_imag = rotate_rows(
        cosine * hits[:, None], sine * hits[:, None], plane[:4], plane[4:]
    )
    return lax.psum_scatter(
        rotate_columns(part_real, part_imag, cosine_v, sine_v) * scale,
        ("gx", "gy"),
        scatter_dimension=0,
        tiled=True,
    )


def shards(fields, adjoint, permittivity, lists, mask):
    update_scale = TIME_STEP / permittivity
    forward = [member[0] for member in sweep(fields[None], update_scale)]
    plane = monitor(forward[1], forward[2], forward[3], forward[4])
    farfield = far_field(plane, lists, mask)
    backward = [member[0] for member in sweep(adjoint[None], update_scale)]
    sensitivity = OMEGA**2 * jnp.sum(forward[1] * backward[1] - forward[2] * backward[2], axis=0)
    return (forward[0], backward[0], sensitivity, farfield)


def solution(mesh):
    in_specs = (P(None, None, "gx", "gy"), P(None, None, "gx", "gy"), P(None, "gx", "gy"), P(), P())
    out_specs = (
        P(None, None, "gx", "gy"),
        P(None, None, "gx", "gy"),
        P(None, "gx", "gy"),
        P(("gx", "gy"), None, None),
    )
    return jax.shard_map(shards, mesh=mesh, in_specs=in_specs, out_specs=out_specs, check_vma=False)
```

profile of v0, /device:TPU:1, one launch (start us, length us, event | category | flops | bytes accessed | tf_op | source)
XLA Modules:
  0.0 1437.7 jit_solution(18042706574099744629)
XLA Ops:
  7.2 1.5 copy.749
  10.9 5.2 collective-permute-start.1
  16.1 1.5 copy.748
  17.6 1.3 collective-permute-start.8
  19.8 1.9 collective-permute-start.9
  23.9 1.7 slice_bitcast_fusion.44
  46.3 5.5 collective-permute-start.3
  54.0 3.9 collective-permute-start.2
  58.0 1.6 fusion.45
  62.2 3.4 collective-permute-start.11
  66.1 2.2 collective-permute-start.10
  73.4 1.5 fusion.20
  75.9 2.2 collective-permute-start.5
  88.3 2.4 collective-permute-done.4
  90.7 1.5 fusion.28
  93.0 3.7 collective-permute-start.7
  97.1 5.3 collective-permute-start.6
  105.4 1.8 bitcast_dynamic-update-slice_fusion.4
  110.5 2.1 copy_dynamic-update-slice_fusion.3
  113.5 1.9 collective-permute-start.13
  120.8 1.9 collective-permute-done.12
  122.7 1.6 fusion.64
  124.7 4.8 collective-permute-start.14
  129.6 5.2 collective-permute-start.15
  141.7 1.5 fusion.85
  143.2 1.5 fusion.83
  144.7 1.5 fusion.1
  146.3 1.5 fusion
  147.8 1.5 maximum_multiply_fusion
  149.2 3.1 copy.688
  153.7 1.4 copy.689
  157.9 1273.0 %reduce-scatter.2.cloned.1.call-done = f32[1,8,256]{2,1,0:T(8,128)} async-done(((f32[256,8,256]{2,1,0:T(8,128)}), f32[1,8,256]{2,1,0:T(8,128)}) %reduce-scatter.2.cloned.1.call-update) | async-done | bytes 8208 | tf_op jit(solution)/shard_map/reduce_scatter | solution.py:181
  (266 shorter events, 71.4 us)
Async XLA Ops:
  7.2 16.6 %copy-start = (s32[256,128]{1,0:T(8,128)S(1)}, s32[256,128]{1,0:T(8,128)}, u32[]{:S(2)}) copy-start(s32[256,128]{1,0:T(8,128)} %param.8) | copy-start | bytes 393220
  7.2 1423.7 %reduce-scatter.2.cloned.1.call-start = ((), (), s32[]{:S(2)}) async-start(), calls=%async_computation.1 | async-start | bytes 2105344 | tf_op jit(solution)/shard_map/reduce_scatter | solution.py:181
  9.4 27.2 %collective-permute-start = (f32[1,2,48,128]{3,2,1,0:T(8,128)}, f32[1,2,48,128]{3,2,1,0:T(8,128)}, u32[]{:S(2)}, u32[]{:S(2)}) collective-permute-start(f32[1,2,48,128]{3,2,1,0:T(8,128)} %slice_bitcast_fusion.10), channel_id=1, source_target_pairs={{16,0},{32,16},{48,32},{64,48},{80,64},{96,80},{112,96},{128,112},... | collective-permute-start | bytes 147464 | tf_op jit(solution)/shard_map/ppermute | solution.py:22
  10.9 20.0 %collective-permute-start.1 = (f32[1,2,48,8]{2,3,1,0:T(8,128)S(1)}, f32[1,2,48,8]{2,3,1,0:T(8,128)}, u32[]{:S(2)}, u32[]{:S(2)}) collective-permute-start(f32[1,2,48,8]{2,3,1,0:T(8,128)S(1)} %bitcast.382), channel_id=1, source_target_pairs={{1,0},{2,1},{3,2},{4,3},{5,4},{6,5},{7,6},{8,7},{9,8},{10,9},{11,1... | collective-permute-start | bytes 9224 | tf_op jit(solution)/shard_map/ppermute | solution.py:22
  17.6 22.3 %collective-permute-start.8 = (f32[1,2,48,128]{3,2,1,0:T(8,128)S(1)}, f32[1,2,48,128]{3,2,1,0:T(8,128)}, u32[]{:S(2)}, u32[]{:S(2)}) collective-permute-start(f32[1,2,48,128]{3,2,1,0:T(8,128)S(1)} %slice_bitcast_fusion.9), channel_id=1, source_target_pairs={{16,0},{32,16},{48,32},{64,48},{80,64},{96,80},{112,96},{128,112},... | collective-permute-start | bytes 147464 | tf_op jit(solution)/shard_map/ppermute | solution.py:22
  19.0 4.9 copy-start.1
  19.8 11.8 collective-permute-start.9
  22.5 7.1 copy-start.11
  22.5 7.8 copy-start.14
  23.9 4.9 copy-start.18
  39.9 12.0 copy-start.9
  46.3 26.1 %collective-permute-start.3 = (f32[1,2,48,128]{3,1,2,0:T(2,128)}, f32[1,2,48,128]{3,1,2,0:T(2,128)}, u32[]{:S(2)}, u32[]{:S(2)}) collective-permute-start(f32[1,2,48,128]{3,1,2,0:T(2,128)} %bitcast.24), channel_id=1, source_target_pairs={{0,16},{16,32},{32,48},{48,64},{64,80},{80,96},{96,112},{112,128},... | collective-permute-start | bytes 147464 | tf_op jit(solution)/shard_map/ppermute | solution.py:22
  51.9 6.0 copy-start.38
  54.0 14.2 collective-permute-start.2
  62.2 16.6 %collective-permute-start.11 = (f32[1,2,48,128]{3,2,1,0:T(8,128)S(1)}, f32[1,2,48,128]{3,2,1,0:T(8,128)}, u32[]{:S(2)}, u32[]{:S(2)}) collective-permute-start(f32[1,2,48,128]{3,2,1,0:T(8,128)S(1)} %fusion.93), channel_id=1, source_target_pairs={{0,16},{16,32},{32,48},{48,64},{64,80},{80,96},{96,112},{112,128},... | collective-permute-start | bytes 147464 | tf_op jit(solution)/shard_map/ppermute | solution.py:22
  65.7 7.6 copy-start.3
  65.7 7.6 copy-start.25
  66.1 3.1 collective-permute-start.10
  75.9 4.8 copy-start.12
  75.9 10.7 collective-permute-start.5
  85.3 5.3 collective-permute-start.4
  92.3 4.5 copy-start.10
  93.0 15.8 %collective-permute-start.7 = (f32[1,2,48,128]{3,2,1,0:T(8,128)}, f32[1,2,48,128]{3,2,1,0:T(8,128)}, u32[]{:S(2)}, u32[]{:S(2)}) collective-permute-start(f32[1,2,48,128]{3,2,1,0:T(8,128)} %fusion.94), channel_id=1, source_target_pairs={{0,16},{16,32},{32,48},{48,64},{64,80},{80,96},{96,112},{112,128},... | collective-permute-start | bytes 147464 | tf_op jit(solution)/shard_map/ppermute | solution.py:22
  97.1 7.4 collective-permute-start.6
  105.4 5.1 copy-start.8
  105.4 5.1 copy-start.15
  105.4 5.1 copy-start.21
  113.5 5.7 collective-permute-start.13
  116.2 6.5 copy-start.24
  117.9 4.8 collective-permute-start.12
  124.7 10.1 collective-permute-start.14
  129.6 7.0 collective-permute-start.15
  (30 other events, 61.8 us)
Sparse Core Ops, SparseCore 0:
  152.5 1278.3 reduce-scatter.1
where the time goes:
time: 1440 us
  waiting for transfers between devices  1280 us (89%)
  local copies, waits for them, and re-layouts  62.5 us (4%)
  starting transfers between devices  50.4 us (4%)
  other arithmetic  22.8 us (2%)
  between operations  15.8 us (1%)
    reduce_scatter x1, waiting for transfers between devices, far_field(): lax.psum_scatter(rotate_columns(part_real, part_imag, cosine_v, sine_v) *...  1270 us
    ppermute x16, starting transfers between devices, shifted(): lax.ppermute(value, axis, [(source, source + steps) for source in range(i...  50.4 us
  transfers between devices with their start and end apart: 17, of which 4 were waited for; matrix products, arithmetic and copies ran while one was open for 4% of the time, Pallas kernels for 0%

commit v1 on v0

v1 whole, which is shorter than its diff:
```python
import functools
import math

import jax
import jax.numpy as jnp
from jax import lax
from jax.experimental import pallas as pl
from jax.experimental.pallas import tpu as pltpu
from jax.sharding import PartitionSpec as P

NZ, CX, CY = 48, 8, 128
ROWS = NZ * CX
ZM = 36
Z0 = ZM - 2
TIME_STEP = 0.5
PHASE_STEP = 0.3
OMEGA = PHASE_STEP / TIME_STEP
HIGHEST = lax.Precision.HIGHEST
MESH = pl.DeviceIdType.MESH
F32 = jnp.float32
NB = NZ // 8

ROWS_UP = [(c, 0) for c in range(6)] + [(1, 1), (2, 1), (6, 0)]
ROWS_DOWN = [(c, 7) for c in range(6)] + [(c, 6) for c in (0, 1, 2, 4, 5)] + [(6, 7)]
TILES_Y = (
    [(c, z) for c in range(3) for z in range(Z0, Z0 + 5)]
    + [(c, z) for c in range(3, 6) for z in range(Z0, Z0 + 4)]
    + [(6, z) for z in range(Z0 + 1, Z0 + 4)]
)


def weights_at(moment):
    theta = PHASE_STEP * moment
    return (math.cos(theta) * TIME_STEP, -math.sin(theta) * TIME_STEP)


def cos_turns(m):
    m = m + 512
    quarter = (m >> 10) & 3
    angle = ((m & 1023) - 512).astype(F32) * (2.0 * math.pi / 4096)
    a2 = angle * angle
    cosine = 1.0 + a2 * (-0.5 + a2 * (1 / 24 + a2 * (-1 / 720 + a2 * (1 / 40320))))
    sine = angle * (1.0 + a2 * (-1 / 6 + a2 * (1 / 120 + a2 * (-1 / 5040 + a2 * (1 / 362880)))))
    value = jnp.where((quarter & 1) == 1, sine, cosine)
    return jnp.where(((quarter + 1) & 2) == 2, -value, value)


def iota(shape, axis):
    return lax.broadcasted_iota(jnp.int32, shape, axis)


def wide(row):
    return jnp.broadcast_to(row, (8, 128))


def kernel(
    dims,
    f_ref, a_ref, eps_ref, lists_ref, mask_ref,
    fo_ref, ao_ref, sens_ref, far_ref,
    scale, xs, xr, ys, yr,
    up_s, down_s, col_s, cor_s, up_r, down_r, col_r, cor_r, dup, ddown,
    gath, wtab, vtab, tws, part, part_r, total, rows_s, rows_r,
    send_sem, recv_sem,
):
    n_zh, n_xi, n_gy = dims
    n_gx = n_zh * n_xi
    gx = lax.axis_index("gx")
    gy = lax.axis_index("gy")
    zh = gx // n_xi
    xi = gx % n_xi

    def dev(dx, dy):
        return {"gx": (gx + (dx + n_gx)) % n_gx, "gy": (gy + (dy + n_gy)) % n_gy}

    def zh_peer(d):
        return {"gx": ((zh + d) % n_zh) * n_xi + xi, "gy": gy}

    def xi_peer(d):
        return {"gx": zh * n_xi + (xi + d) % n_xi, "gy": gy}

    barrier = pltpu.get_barrier_semaphore()
    peers = [dev(dx, dy) for dx in (-1, 1) for dy in (-1, 0, 1)]
    peers += [zh_peer(d) for d in range(1, n_zh)] + [xi_peer(d) for d in range(1, n_xi)]
    for peer in peers:
        pl.semaphore_signal(barrier, inc=1, device_id=peer, device_id_type=MESH)

    def greet(d, carry):
        pl.semaphore_signal(
            barrier, inc=1, device_id={"gx": gx, "gy": (gy + d) % n_gy}, device_id_type=MESH
        )
        return carry

    lax.fori_loop(1, n_gy, greet, 0)

    started = []

    def send(src, dst, slot, peer):
        copy = pltpu.make_async_remote_copy(
            src_ref=src, dst_ref=dst, send_sem=send_sem.at[slot], recv_sem=recv_sem.at[slot],
            device_id=peer, device_id_type=MESH,
        )
        copy.start()
        started.append(copy)
        return copy

    row = iota((8, 128), 0)
    lane = iota((8, 128), 1)

    def layer(c, r, ref=f_ref):
        if c == 6:
            return eps_ref[pl.ds(Z0 * 8 + r, 8, stride=8), :]
        return ref[pl.ds(c * ROWS + Z0 * 8 + r, 8, stride=8), :]

    def tile(c, z):
        if c == 6:
            return eps_ref[z * 8 : z * 8 + 8, :]
        return f_ref[c * ROWS + z * 8 : c * ROWS + z * 8 + 8, :]

    def packed(values, low):
        out = jnp.zeros((8, 128), F32)
        for k, value in enumerate(values):
            shift = (2 * k if low else 2 * k + 2) % 128
            moved = pltpu.roll(value, shift, 1) if shift else value
            out = jnp.where((lane >> 1) == k, moved, out)
        return out

    def unpacked(low, high, k):
        first = pltpu.roll(low, (128 - 2 * k) % 128, 1) if k else low
        second = pltpu.roll(high, (126 - 2 * k) % 128, 1)
        return jnp.where(lane < 64, first, second)

    ups = [layer(c, r) for c, r in ROWS_UP]
    downs = [layer(c, r) for c, r in ROWS_DOWN]
    for k, value in enumerate(ups):
        up_s[k * 8 : k * 8 + 8, :] = value
    for k, value in enumerate(downs):
        down_s[k * 8 : k * 8 + 8, :] = value
    cor_s[0:8, :] = packed(ups, True)
    cor_s[8:16, :] = packed(ups, False)
    cor_s[16:24, :] = packed(downs, True)
    cor_s[24:32, :] = packed(downs, False)
    tiles_y = [tile(c, z) for c, z in TILES_Y]
    col_s[0:8, :] = packed(tiles_y, True)
    col_s[8:16, :] = packed(tiles_y, False)

    def at(ref, c, b, j):
        return ref[pl.ds(pl.multiple_of(c * ROWS + b * 64 + j * 8, 8), 8), :]

    def put(ref, c, b, j, value):
        ref[pl.ds(pl.multiple_of(c * ROWS + b * 64 + j * 8, 8), 8), :] = value

    def slot_of(step, state):
        return step * 2 + state

    def x_rows(ref, comps, r, slot):
        for n, c in enumerate(comps):
            xs[slot, n * NZ : n * NZ + NZ, :] = ref[pl.ds(c * ROWS + r, NZ, stride=8), :]

    def join(acc, new, b):
        moved = pltpu.roll(new, b * 8, 1)
        return jnp.where((lane >> 3) == b, moved, acc)

    def send_pair(slot, ahead):
        step = -1 if ahead else 1
        return (
            send(xs.at[slot], xr.at[slot], slot, dev(step, 0)),
            send(ys.at[slot], yr.at[slot], 8 + slot, dev(0, step)),
        )

    zero = jnp.zeros((8, 128), F32)

    def first_columns(ref, slot):
        def body(b, accs):
            out = []
            for acc, c in zip(accs, (0, 2)):
                new = zero
                for j in range(8):
                    value = at(ref, c, b, j)
                    new = jnp.where(lane == j, pltpu.roll(value, j, 1) if j else value, new)
                out.append(join(acc, new, b))
            return tuple(out)

        low, high = lax.fori_loop(0, NB, body, (zero, zero))
        ys[slot, 0:8, :] = low
        ys[slot, 8:16, :] = high

    refs_in = (f_ref, a_ref)
    refs_out = (fo_ref, ao_ref)
    for s in range(2):
        x_rows(refs_in[s], (1, 2), 0, slot_of(0, s))
        first_columns(refs_in[s], slot_of(0, s))

    pl.semaphore_wait(barrier, len(peers) + n_gy - 1)

    base = 16
    a_copies = [
        send(up_s, up_r, base + 0, dev(-1, 0)),
        send(down_s, down_r, base + 1, dev(1, 0)),
        send(col_s.at[0:8], col_r.at[0:8], base + 2, dev(0, -1)),
        send(col_s.at[8:16], col_r.at[8:16], base + 3, dev(0, 1)),
        send(cor_s.at[0:8], cor_r.at[0:8], base + 4, dev(-1, -1)),
        send(cor_s.at[8:16], cor_r.at[8:16], base + 5, dev(-1, 1)),
        send(cor_s.at[16:24], cor_r.at[16:24], base + 6, dev(1, -1)),
        send(cor_s.at[24:32], cor_r.at[24:32], base + 7, dev(1, 1)),
    ]
    pending = {}
    for s in range(2):
        pending[slot_of(0, s)] = send_pair(slot_of(0, s), True)

    def scales(b, carry):
        rows = pl.ds(pl.multiple_of(b * 64, 64), 64)
        scale[rows, :] = 0.5 / eps_ref[rows, :]
        return carry

    lax.fori_loop(0, NB, scales, 0)

    n_w = n_xi * 2 * n_gy
    n_k = n_zh * 16
    wrow = iota((n_w, 128), 0)
    wlane = iota((n_w, 128), 1)
    u = zh * (n_xi * n_gy) + (wrow // (2 * n_gy)) * n_gy + wrow % n_gy
    imag_out = (wrow // n_gy) % 2
    back = wlane // 16
    imag_in = (wlane // 8) % 2
    x = (((zh - back + n_zh) % n_zh) * n_xi + xi) * 8 + wlane % 8
    n_u = n_gx * n_gy
    weights = cos_turns((2 * u + 1 - n_u) * x * (4096 // (16 * n_u)) + 1024 * (imag_out - imag_in))
    hits = jnp.zeros((n_w, 128), F32)
    for d in range(n_zh):
        t = (((zh - d + n_zh) % n_zh) * n_xi + xi) * n_gy + gy
        same = (lists_ref[pl.ds(t, 1), :] == u[:, : lists_ref.shape[1]]).astype(F32)
        count = jnp.sum(same, axis=1, keepdims=True) * mask_ref[t].astype(F32)
        hits = jnp.where(back == d, count, hits)
    wtab[...] = weights * hits

    def v_rows(b, carry):
        y = b * 8 + iota((8, 512), 0)
        v = iota((8, 512), 1)
        vtab[pl.ds(pl.multiple_of(b * 8, 8), 8), :] = cos_turns(
            (2 * (v & 255) - 255) * y - 1024 * (v >> 8)
        )
        return carry

    lax.fori_loop(0, 16, v_rows, 0)
    d = iota((n_gy, 512), 0)
    v = iota((n_gy, 512), 1)
    tws[...] = cos_turns((2 * (v & 255) - 255) * (((gy - d + n_gy) % n_gy) * 128) - 1024 * (v >> 8))

    for copy in a_copies:
        copy.wait_recv()

    for k in range(len(ROWS_UP)):
        dup[k * 8 : k * 8 + 8, :] = unpacked(cor_r[0:8, :], cor_r[8:16, :], k)
    for k in range(len(ROWS_DOWN)):
        ddown[k * 8 : k * 8 + 8, :] = unpacked(cor_r[16:24, :], cor_r[24:32, :], k)

    far_row = gx * 8 + jnp.where(row < 4, row + 8, row - 8)
    far_lane = gy * 128 + jnp.where(lane < 64, lane + 128, lane - 128)
    row_in = (far_row >= 0) & (far_row < n_gx * 8)
    lane_in = (far_lane >= 0) & (far_lane < n_gy * 128)
    inside = [[None, lane_in], [row_in, row_in & lane_in]]
    where_up = {key: k for k, key in enumerate(ROWS_UP)}
    where_down = {key: k for k, key in enumerate(ROWS_DOWN)}

    def border_rows(up, down, c, z):
        o = z - Z0

        def get(ref, k):
            return wide(ref[k * 8 + o : k * 8 + o + 1, :])

        up0, down0 = get(up, where_up[(c, 0)]), get(down, where_down[(c, 7)])
        out = jnp.where(row < 4, up0, down0)
        if (c, 1) in where_up:
            out = jnp.where(row == 1, get(up, where_up[(c, 1)]), out)
        if (c, 6) in where_down:
            out = jnp.where(row == 6, get(down, where_down[(c, 6)]), out)
        return out

    def masked(q, other=0.0):
        return [
            [q[r][n] if inside[r][n] is None else jnp.where(inside[r][n], q[r][n], other) for n in range(2)]
            for r in range(2)
        ]

    def extended(c, z):
        k = TILES_Y.index((c, z))
        q = [
            [tile(c, z), unpacked(col_r[0:8, :], col_r[8:16, :], k)],
            [border_rows(up_r, down_r, c, z), border_rows(dup, ddown, c, z)],
        ]
        return masked(q, 1.0 if c == 6 else 0.0)

    def combine(fn, *qs):
        return [[fn(*[q[r][n] for q in qs]) for n in range(2)] for r in range(2)]

    def turn_x(q, shift, edge):
        out = [[None, None], [None, None]]
        for n in range(2):
            first, second = pltpu.roll(q[0][n], shift, 0), pltpu.roll(q[1][n], shift, 0)
            out[0][n] = jnp.where(row == edge, second, first)
            out[1][n] = jnp.where(row == edge, first, second)
        return out

    def turn_y(q, shift, edge):
        out = []
        for r in range(2):
            first, second = pltpu.roll(q[r][0], shift, 1), pltpu.roll(q[r][1], shift, 1)
            out.append([jnp.where(lane == edge, second, first), jnp.where(lane == edge, first, second)])
        return out

    def ahead_x(q):
        return combine(jnp.subtract, turn_x(q, 7, 7), q)

    def ahead_y(q):
        return combine(jnp.subtract, turn_y(q, 127, 127), q)

    def behind_x(q):
        return combine(jnp.subtract, q, turn_x(q, 1, 0))

    def behind_y(q):
        return combine(jnp.subtract, q, turn_y(q, 1, 0))

    def half(h, one, two):
        return masked(combine(lambda h, p, q: h - TIME_STEP * (p - q), h, one, two))

    def full(e, us, one, two):
        return masked(combine(lambda e, us, p, q: e + us * (p - q), e, us, one, two))

    def minus(p, q):
        return combine(jnp.subtract, p, q)

    def magnetic(e, h, zs):
        for z in zs:
            ex, ey, ez = (e[(c, z)] for c in range(3))
            h[(3, z)] = half(h[(3, z)], ahead_y(ez), minus(e[(1, z + 1)], ey))
            h[(4, z)] = half(h[(4, z)], minus(e[(0, z + 1)], ex), ahead_x(ez))
            h[(5, z)] = half(h[(5, z)], ahead_x(ey), ahead_y(ex))

    e = {(c, z): extended(c, z) for c, z in TILES_Y if c < 3}
    h = {(c, z): extended(c, z) for c, z in TILES_Y if 3 <= c < 6}
    us = {z: combine(lambda p: 0.5 / p, extended(6, z)) for c, z in TILES_Y if c == 6}
    magnetic(e, h, range(Z0, Z0 + 4))
    h1 = [h[(3, ZM)][0][0], h[(4, ZM)][0][0]]
    for z in range(Z0 + 1, Z0 + 4):
        hx, hy, hz = (h[(c, z)] for c in (3, 4, 5))
        e[(0, z)] = full(e[(0, z)], us[z], behind_y(hz), minus(hy, h[(4, z - 1)]))
        e[(1, z)] = full(e[(1, z)], us[z], minus(hx, h[(3, z - 1)]), behind_x(hz))
        e[(2, z)] = full(e[(2, z)], us[z], behind_x(hy), behind_y(hx))
    e1 = [e[(0, ZM)][0][0], e[(1, ZM)][0][0]]
    magnetic(e, h, range(Z0 + 1, Z0 + 3))
    h2 = [h[(3, ZM)][0][0], h[(4, ZM)][0][0]]
    hz = h[(5, ZM)]
    us_m = us[ZM][0][0]
    e2 = [
        e1[0] + us_m * (behind_y(hz)[0][0] - (h2[1] - h[(4, ZM - 1)][0][0])),
        e1[1] + us_m * ((h2[0] - h[(3, ZM - 1)][0][0]) - behind_x(hz)[0][0]),
    ]
    for part_of in range(2):
        first, second = weights_at(0.5)[part_of], weights_at(1.5)[part_of]
        hx, hy = (first * h1[n] + second * h2[n] for n in range(2))
        first, second = weights_at(1)[part_of], weights_at(2)[part_of]
        ex, ey = (first * e1[n] + second * e2[n] for n in range(2))
        for n, value in enumerate((-hy, hx, ey, -ex)):
            gath[0, (part_of * 4 + n) * 8 : (part_of * 4 + n) * 8 + 8, :] = value

    base_g = base + 8
    g_copies = [send(gath.at[0], gath.at[d], base_g + d - 1, zh_peer(d)) for d in range(1, n_zh)]

    def arrived(slot, ahead):
        for copy in pending[slot]:
            copy.wait_recv()
        last_x = n_gx - 1 if ahead else 0
        last_y = n_gy - 1 if ahead else 0

        @pl.when(gx == last_x)
        def _():
            xr[slot] = jnp.zeros((2 * NZ, 128), F32)

        @pl.when(gy == last_y)
        def _():
            yr[slot] = jnp.zeros((16, 128), F32)

    def magnetic_step(step, s, src, dst):
        got = slot_of(step, s)
        out = slot_of(step + 1, s)
        arrived(got, True)

        def body(b, accs):
            sides = [pltpu.roll(yr[got, n * 8 : n * 8 + 8, :], 120 - 8 * b, 1) for n in range(2)]
            news = [zero, zero]
            ex, ey, ez = (at(src, c, b, 0) for c in range(3))
            for j in range(8):
                nex, ney = at(src, 0, b, j + 1), at(src, 1, b, j + 1)
                if j == 7:
                    nex, ney = jnp.where(b < NB - 1, nex, 0.0), jnp.where(b < NB - 1, ney, 0.0)

                def along_y(value, n, j=j):
                    side = pltpu.roll(sides[n], 7 - j, 1) if j < 7 else sides[n]
                    return jnp.where(lane == 127, side, pltpu.roll(value, 127, 1)) - value

                def along_x(value, n, j=j):
                    side = wide(xr[got, pl.ds(n * NZ + b * 8 + j, 1), :])
                    return jnp.where(row == 7, side, pltpu.roll(value, 7, 0)) - value

                hx = at(src if step == 0 else dst, 3, b, j) - TIME_STEP * (along_y(ez, 1) - (ney - ey))
                hy = at(src if step == 0 else dst, 4, b, j) - TIME_STEP * ((nex - ex) - along_x(ez, 1))
                hz = at(src if step == 0 else dst, 5, b, j) - TIME_STEP * (along_x(ey, 0) - along_y(ex, 0))
                for n, value in enumerate((hx, hy, hz)):
                    put(dst, 3 + n, b, j, value)
                for n, value in enumerate((hx, hz)):
                    news[n] = jnp.where(lane == j, pltpu.roll(value, 1 + j, 1), news[n])
                if j < 7:
                    ex, ey, ez = nex, ney, at(src, 2, b, j + 1)
            return tuple(join(acc, new, b) for acc, new in zip(accs, news))

        low, high = lax.fori_loop(0, NB, body, (zero, zero))
        ys[out, 0:8, :] = low
        ys[out, 8:16, :] = high
        x_rows(dst, (4, 5), 7, out)
        pending[out] = send_pair(out, False)

    def electric_block(step, s, src, dst, b, each):
        got = slot_of(step, s)
        sides = [pltpu.roll(yr[got, n * 8 : n * 8 + 8, :], (128 - 8 * b) % 128, 1) for n in range(2)]
        phx, phy = at(dst, 3, b, -1), at(dst, 4, b, -1)
        phx, phy = jnp.where(b > 0, phx, 0.0), jnp.where(b > 0, phy, 0.0)
        for j in range(8):
            hx, hy, hz = (at(dst, c, b, j) for c in (3, 4, 5))

            def along_y(value, n, j=j):
                side = pltpu.roll(sides[n], 128 - j, 1) if j else sides[n]
                return value - jnp.where(lane == 0, side, pltpu.roll(value, 1, 1))

            def along_x(value, n, j=j):
                side = wide(xr[got, pl.ds(n * NZ + b * 8 + j, 1), :])
                return value - jnp.where(row == 0, side, pltpu.roll(value, 1, 0))

            us = at(scale, 0, b, j)
            old = [at(src, c, b, j) for c in range(3)]
            ex = old[0] + us * (along_y(hz, 1) - (hy - phy))
            ey = old[1] + us * ((hx - phx) - along_x(hz, 1))
            ez = old[2] + us * (along_x(hy, 0) - along_y(hx, 0))
            for n, value in enumerate((ex, ey, ez)):
                put(dst, n, b, j, value)
            each(j, old, [ex, ey, ez])
            phx, phy = hx, hy

    def electric_step(step, s, src, dst):
        out = slot_of(step + 1, s)
        arrived(slot_of(step, s), False)

        def body(b, accs):
            news = [zero, zero]

            def each(j, old, new):
                for n, value in enumerate((new[0], new[2])):
                    news[n] = jnp.where(lane == j, pltpu.roll(value, j, 1) if j else value, news[n])

            electric_block(step, s, src, dst, b, each)
            return tuple(join(acc, new, b) for acc, new in zip(accs, news))

        low, high = lax.fori_loop(0, NB, body, (zero, zero))
        ys[out, 0:8, :] = low
        ys[out, 8:16, :] = high
        x_rows(dst, (1, 2), 0, out)
        pending[out] = send_pair(out, True)

    def last_step():
        for s in range(2):
            arrived(slot_of(3, s), False)
        (a1, b1), (a2, b2) = weights_at(1), weights_at(2)
        k11, k12, k22 = (OMEGA**2 * k for k in (a1 * a1 - b1 * b1, a1 * a2 - b1 * b2, a2 * a2 - b2 * b2))

        def body(b, carry):
            seen = {}

            def each_forward(j, old, new):
                seen[j] = (
                    [k11 * p + k12 * q for p, q in zip(old, new)],
                    [k12 * p + k22 * q for p, q in zip(old, new)],
                )

            def each_adjoint(j, old, new):
                first, second = seen[j]
                terms = [p * w + q * z for p, q, w, z in zip(old, new, first, second)]
                put(sens_ref, 0, b, j, terms[0] + terms[1] + terms[2])

            electric_block(3, 0, fo_ref, fo_ref, b, each_forward)
            electric_block(3, 1, ao_ref, ao_ref, b, each_adjoint)
            return carry

        lax.fori_loop(0, NB, body, 0)

    for s in range(2):
        magnetic_step(0, s, refs_in[s], refs_out[s])

    for copy in g_copies:
        copy.wait_recv()
    table = wtab[:, 0:n_k]
    blk = 8 * n_gy
    for c in range(4):
        planes = jnp.concatenate(
            [gath[d, (4 * r + c) * 8 : (4 * r + c) * 8 + 8, :] for d in range(n_zh) for r in range(2)], axis=0
        )
        out = jnp.dot(table, planes, preferred_element_type=F32, precision=HIGHEST)
        for q in range(n_xi):
            for r in range(2):
                part[q * blk + r * 4 * n_gy + c * n_gy : q * blk + r * 4 * n_gy + (c + 1) * n_gy, :] = out[
                    (q * 2 + r) * n_gy : (q * 2 + r + 1) * n_gy, :
                ]
    base_r = base_g + n_zh - 1
    r_copies = []
    for d in range(1, n_xi):
        to = (xi + d) % n_xi
        r_copies.append(
            send(
                part.at[pl.ds(pl.multiple_of(to * blk, blk), blk)], part_r.at[d - 1], base_r + d - 1, xi_peer(d)
            )
        )

    for s in range(2):
        electric_step(1, s, refs_in[s], refs_out[s])

    for copy in r_copies:
        copy.wait_recv()
    acc = part[pl.ds(pl.multiple_of(xi * blk, blk), blk), :]
    for d in range(1, n_xi):
        acc = acc + part_r[d - 1]
    total[...] = acc
    for j in range(n_gy):
        rows_s[j] = total[pl.ds(j, 8, stride=n_gy), :]
    rows_r[0] = rows_s[gy]
    base_a = base_r + n_xi - 1
    last_copies = []
    for d in range(1, n_gy):
        to = (gy + d) % n_gy
        last_copies.append(
            send(rows_s.at[to], rows_r.at[d], base_a + d - 1, {"gx": gx, "gy": to})
        )

    for s in range(2):
        magnetic_step(2, s, refs_out[s], refs_out[s])

    for copy in last_copies:
        copy.wait_recv()
    turned = jnp.dot(
        rows_r[...].reshape(n_gy * 8, 128), vtab[...], preferred_element_type=F32, precision=HIGHEST
    )
    sign = jnp.where(iota((8, 256), 0) < 4, 1.0, -1.0)
    out = jnp.zeros((8, 256), F32)
    for d in range(n_gy):
        rows = turned[d * 8 : d * 8 + 8, :]
        value = rows[:, :256] + sign * pltpu.roll(rows[:, 256:], 4, 0)
        out = out + tws[d : d + 1, :256] * value + tws[d : d + 1, 256:] * (sign * pltpu.roll(value, 4, 0))
    far_ref[...] = out * (1.0 / math.sqrt(CX * CY))

    last_step()

    for copy in started:
        copy.wait_send()


def solution(mesh):
    n_gx, n_gy = mesh.shape["gx"], mesh.shape["gy"]
    n_xi = 4 if n_gx == 16 else n_gx
    dims = (n_gx // n_xi, n_xi, n_gy)
    n_zh = dims[0]
    n_sem = 16 + 8 + (n_zh - 1) + (n_xi - 1) + (n_gy - 1)
    vmem = pl.BlockSpec(memory_space=pltpu.VMEM)
    blk = 8 * n_gy

    def buffer(*shape):
        return pltpu.VMEM(shape, F32)

    def shards(fields, adjoint, permittivity, lists, mask):
        out = pl.pallas_call(
            functools.partial(kernel, dims),
            out_shape=(
                jax.ShapeDtypeStruct((6 * ROWS, 128), F32),
                jax.ShapeDtypeStruct((6 * ROWS, 128), F32),
                jax.ShapeDtypeStruct((ROWS, 128), F32),
                jax.ShapeDtypeStruct((8, 256), F32),
            ),
            in_specs=[vmem] * 4 + [pl.BlockSpec(memory_space=pltpu.SMEM)],
            out_specs=(vmem,) * 4,
            scratch_shapes=[
                buffer(ROWS, 128),
                buffer(8, 2 * NZ, 128), buffer(8, 2 * NZ, 128), buffer(8, 16, 128), buffer(8, 16, 128),
                buffer(72, 128), buffer(96, 128), buffer(16, 128), buffer(32, 128),
                buffer(72, 128), buffer(96, 128), buffer(16, 128), buffer(32, 128),
                buffer(72, 128), buffer(96, 128),
                buffer(n_zh, 64, 128), buffer(n_xi * 2 * n_gy, 128), buffer(128, 512), buffer(n_gy, 512),
                buffer(n_xi * blk, 128), buffer(max(n_xi - 1, 1), blk, 128), buffer(blk, 128),
                buffer(n_gy, 8, 128), buffer(n_gy, 8, 128),
                pltpu.SemaphoreType.DMA((n_sem,)),
                pltpu.SemaphoreType.DMA((n_sem,)),
            ],
            compiler_params=pltpu.CompilerParams(
                collective_id=0, has_side_effects=True, vmem_limit_bytes=40 * 1024 * 1024
            ),
        )(
            fields.reshape(6 * ROWS, 128),
            adjoint.reshape(6 * ROWS, 128),
            permittivity.reshape(ROWS, 128),
            lists,
            mask,
        )
        return (
            out[0].reshape(fields.shape),
            out[1].reshape(fields.shape),
            out[2].reshape(permittivity.shape),
            out[3].reshape(1, 8, 256),
        )

    in_specs = (P(None, None, "gx", "gy"), P(None, None, "gx", "gy"), P(None, "gx", "gy"), P(), P())
    out_specs = (
        P(None, None, "gx", "gy"),
        P(None, None, "gx", "gy"),
        P(None, "gx", "gy"),
        P(("gx", "gy"), None, None),
    )
    return jax.shard_map(shards, mesh=mesh, in_specs=in_specs, out_specs=out_specs, check_vma=False)
```

time: 1440 us -> 55.4 us (0.04)
  the two profiles are of different devices: /device:TPU:1 before, /device:TPU:32 now
where the time goes in v1:
time: 55.4 us; the launch traced here: 55.2 us
  Pallas kernels  46.2 us (83%)
  local copies, waits for them, and re-layouts  8.34 us (15%)
  between operations  0.65 us (1%)
    pallas_call x1, Pallas kernels, shards(): pl.pallas_call(functools.partial(kernel, dims), out_shape=(jax.ShapeDtype...  46.2 us
    unnamed x14, local copies, waits for them, and re-layouts  8.34 us

profile of v1, /device:TPU:32, one launch (start us, length us, event | category | flops | bytes accessed | tf_op | source)
XLA Modules:
  0.0 55.2 jit_solution(1892668799656535721)
XLA Ops:
  0.6 0.0 copy-start
  0.6 1.3 %copy-done = f32[6,48,8,128]{3,2,1,0:T(8,128)S(1)} copy-done((f32[6,48,8,128]{3,2,1,0:T(8,128)S(1)}, f32[6,48,8,128]{3,2,1,0:T(8,128)}, u32[]{:S(2)}) %copy-start) | copy-done | bytes 1179672
  1.9 0.0 copy-start.1
  1.9 1.3 %copy-done.1 = f32[6,48,8,128]{3,2,1,0:T(8,128)S(1)} copy-done((f32[6,48,8,128]{3,2,1,0:T(8,128)S(1)}, f32[6,48,8,128]{3,2,1,0:T(8,128)}, u32[]{:S(2)}) %copy-start.1) | copy-done | bytes 1179672
  3.2 0.0 copy-start.2
  3.2 0.9 %copy-done.2 = f32[48,8,128]{2,1,0:T(8,128)S(1)} copy-done((f32[48,8,128]{2,1,0:T(8,128)S(1)}, f32[48,8,128]{2,1,0:T(8,128)}, u32[]{:S(2)}) %copy-start.2) | copy-done | bytes 196632
  4.1 0.0 copy-start.3
  4.1 0.9 %copy-done.3 = s32[256,128]{1,0:T(8,128)S(1)} copy-done((s32[256,128]{1,0:T(8,128)S(1)}, s32[256,128]{1,0:T(8,128)}, u32[]{:S(2)}) %copy-start.3) | copy-done | bytes 131096
  5.0 0.0 copy-start.4
  5.0 0.7 %copy-done.4 = s32[256]{0:T(256)S(1)} copy-done((s32[256]{0:T(256)S(1)}, s32[256]{0:T(256)}, u32[]{:S(2)}) %copy-start.4) | copy-done | bytes 1048
  5.7 46.2 %shard_map.84 = (f32[2304,128]{1,0:T(8,128)S(1)}, f32[2304,128]{1,0:T(8,128)S(1)}, f32[384,128]{1,0:T(8,128)S(1)}, f32[8,256]{1,0:T(8,128)S(1)}) custom-call(f32[2304,128]{1,0:T(8,128)S(1)} %bitcast.7, f32[2304,128]{1,0:T(8,128)S(1)} %bitcast.8, f32[384,128]{1,0:T(8,128)S(1)} %bitcast.11, s32[256,128]{1,0:T(8,128)S(1)} %copy-done.3, s32[256]{0:T(256)S(1)} %copy-done.4), custom_call_target="tpu_custom_call" | custom-call | tf_op jit(solution)/shard_map/pallas_call | solution.py:576
  51.9 1.0 %copy.13 = f32[6,48,8,128]{3,2,1,0:T(8,128)} copy(f32[6,48,8,128]{3,2,1,0:T(8,128)S(1)} %bitcast.10) | data formatting | bytes 2359296
  52.9 1.0 %copy.14 = f32[6,48,8,128]{3,2,1,0:T(8,128)} copy(f32[6,48,8,128]{3,2,1,0:T(8,128)S(1)} %bitcast.9) | data formatting | bytes 2359296
  54.0 0.7 %copy.15 = f32[48,8,128]{2,1,0:T(8,128)} copy(f32[48,8,128]{2,1,0:T(8,128)S(1)} %bitcast.12) | data formatting | bytes 393216
  54.6 0.6 %copy.16 = f32[1,8,256]{2,1,0:T(8,128)} copy(f32[1,8,256]{2,1,0:T(8,128)S(1)} %bitcast.13) | data formatting | bytes 16384
Async XLA Ops:
  0.6 1.3 %copy-start = (f32[6,48,8,128]{3,2,1,0:T(8,128)S(1)}, f32[6,48,8,128]{3,2,1,0:T(8,128)}, u32[]{:S(2)}) copy-start(f32[6,48,8,128]{3,2,1,0:T(8,128)} %param.5) | copy-start | bytes 3538948
  1.9 1.3 %copy-start.1 = (f32[6,48,8,128]{3,2,1,0:T(8,128)S(1)}, f32[6,48,8,128]{3,2,1,0:T(8,128)}, u32[]{:S(2)}) copy-start(f32[6,48,8,128]{3,2,1,0:T(8,128)} %param.6) | copy-start | bytes 3538948
  3.2 0.9 %copy-start.2 = (f32[48,8,128]{2,1,0:T(8,128)S(1)}, f32[48,8,128]{2,1,0:T(8,128)}, u32[]{:S(2)}) copy-start(f32[48,8,128]{2,1,0:T(8,128)} %param.7) | copy-start | bytes 589828
  4.1 0.9 %copy-start.3 = (s32[256,128]{1,0:T(8,128)S(1)}, s32[256,128]{1,0:T(8,128)}, u32[]{:S(2)}) copy-start(s32[256,128]{1,0:T(8,128)} %lists_ref.1) | copy-start | bytes 393220
  5.0 0.7 %copy-start.4 = (s32[256]{0:T(256)S(1)}, s32[256]{0:T(256)}, u32[]{:S(2)}) copy-start(s32[256]{0:T(256)} %mask_ref.1) | copy-start | bytes 3076

commit v2 on v1

v2 whole, which is shorter than its diff:
```python
import functools
import math

import jax
import jax.numpy as jnp
from jax import lax
from jax.experimental import pallas as pl
from jax.experimental.pallas import tpu as pltpu
from jax.sharding import PartitionSpec as P

NZ, CX, CY = 48, 8, 128
ROWS = NZ * CX
ZM = 36
Z0 = ZM - 2
TIME_STEP = 0.5
PHASE_STEP = 0.3
OMEGA = PHASE_STEP / TIME_STEP
HIGHEST = lax.Precision.HIGHEST
MESH = pl.DeviceIdType.MESH
F32 = jnp.float32
ZB = 8
NB = NZ // ZB

ROWS_UP = [(c, 0) for c in range(6)] + [(1, 1), (2, 1), (6, 0)]
ROWS_DOWN = [(c, 7) for c in range(6)] + [(c, 6) for c in (0, 1, 2, 4, 5)] + [(6, 7)]
TILES_Y = (
    [(c, z) for c in range(3) for z in range(Z0, Z0 + 5)]
    + [(c, z) for c in range(3, 6) for z in range(Z0, Z0 + 4)]
    + [(6, z) for z in range(Z0 + 1, Z0 + 4)]
)


def weights_at(moment):
    theta = PHASE_STEP * moment
    return (math.cos(theta) * TIME_STEP, -math.sin(theta) * TIME_STEP)


def cos_turns(m):
    m = m + 512
    quarter = (m >> 10) & 3
    angle = ((m & 1023) - 512).astype(F32) * (2.0 * math.pi / 4096)
    a2 = angle * angle
    cosine = 1.0 + a2 * (-0.5 + a2 * (1 / 24 + a2 * (-1 / 720 + a2 * (1 / 40320))))
    sine = angle * (1.0 + a2 * (-1 / 6 + a2 * (1 / 120 + a2 * (-1 / 5040 + a2 * (1 / 362880)))))
    value = jnp.where((quarter & 1) == 1, sine, cosine)
    return jnp.where(((quarter + 1) & 2) == 2, -value, value)


def iota(shape, axis):
    return lax.broadcasted_iota(jnp.int32, shape, axis)


def wide(row):
    return jnp.broadcast_to(row, (8, 128))


def kernel(
    dims,
    f_hbm, a_hbm, eps_hbm, lists_hbm, mask_hbm,
    fo_ref, ao_ref, sens_ref, far_ref,
    eps_ref, lists_ref, mask_ref, scale, own,
    es, er, hs, hr, ys, yr_up, yr_down, cxs, cxr, cys, cyr, hrow,
    up_s, down_s, col_s, cor_s, up_r, down_r, col_r, cor_r, dup, ddown,
    gath, wtab, vtab, tws, part, part_r, total, rows_s, rows_r,
    load_sem, send_sem, recv_sem,
):
    n_zh, n_xi, n_gy = dims
    n_gx = n_zh * n_xi
    gx = lax.axis_index("gx")
    gy = lax.axis_index("gy")
    zh = gx // n_xi
    xi = gx % n_xi

    def dev(dx, dy):
        return {"gx": (gx + (dx + n_gx)) % n_gx, "gy": (gy + (dy + n_gy)) % n_gy}

    def zh_peer(d):
        return {"gx": ((zh + d) % n_zh) * n_xi + xi, "gy": gy}

    def xi_peer(d):
        return {"gx": zh * n_xi + (xi + d) % n_xi, "gy": gy}

    barrier = pltpu.get_barrier_semaphore()
    peers = [dev(dx, dy) for dx in (-1, 1) for dy in (-1, 0, 1)]
    peers += [zh_peer(d) for d in range(1, n_zh)] + [xi_peer(d) for d in range(1, n_xi)]
    for peer in peers:
        pl.semaphore_signal(barrier, inc=1, device_id=peer, device_id_type=MESH)

    def greet(d, carry):
        pl.semaphore_signal(
            barrier, inc=1, device_id={"gx": gx, "gy": (gy + d) % n_gy}, device_id_type=MESH
        )
        return carry

    lax.fori_loop(1, n_gy, greet, 0)

    def load(src, dst, slot):
        copy = pltpu.make_async_copy(src, dst, load_sem.at[slot])
        copy.start()
        return copy

    def tile_of(d):
        return (((zh - d + n_zh) % n_zh) * n_xi + xi) * n_gy + gy

    load_f = load(f_hbm, fo_ref, 0)
    load_eps = load(eps_hbm, eps_ref, 1)
    load_a = load(a_hbm, ao_ref, 2)
    load_rest = [load(mask_hbm, mask_ref, 3)]
    for d in range(n_zh):
        first = pl.multiple_of(tile_of(d) // 8 * 8, 8)
        load_rest.append(load(lists_hbm.at[pl.ds(first, 8)], lists_ref.at[d], 4 + d))

    started = []

    def send(src, dst, slot, peer):
        copy = pltpu.make_async_remote_copy(
            src_ref=src, dst_ref=dst, send_sem=send_sem.at[slot], recv_sem=recv_sem.at[slot],
            device_id=peer, device_id_type=MESH,
        )
        copy.start()
        started.append(copy)
        return copy

    row = iota((8, 128), 0)
    lane = iota((8, 128), 1)
    zero = jnp.zeros((8, 128), F32)

    def layer(c, r):
        if c == 6:
            return eps_ref[pl.ds(Z0 * 8 + r, 8, stride=8), :]
        return fo_ref[pl.ds(c * ROWS + Z0 * 8 + r, 8, stride=8), :]

    def packed(values, low):
        out = zero
        for k, value in enumerate(values):
            shift = (2 * k if low else 2 * k + 2) % 128
            moved = pltpu.roll(value, shift, 1) if shift else value
            out = jnp.where((lane >> 1) == k, moved, out)
        return out

    def unpacked(low, high, k):
        first = pltpu.roll(low, (128 - 2 * k) % 128, 1) if k else low
        second = pltpu.roll(high, (126 - 2 * k) % 128, 1)
        return jnp.where(lane < 64, first, second)

    load_f.wait()
    load_eps.wait()
    ups = [layer(c, r) for c, r in ROWS_UP]
    downs = [layer(c, r) for c, r in ROWS_DOWN]
    for k, value in enumerate(ups):
        up_s[k * 8 : k * 8 + 8, :] = value
    for k, value in enumerate(downs):
        down_s[k * 8 : k * 8 + 8, :] = value
    cor_s[0:8, :] = packed(ups, True)
    cor_s[8:16, :] = packed(ups, False)
    cor_s[16:24, :] = packed(downs, True)
    cor_s[24:32, :] = packed(downs, False)
    tiles_y = []
    for k, (c, z) in enumerate(TILES_Y):
        at_z = z * 8 if c == 6 else c * ROWS + z * 8
        value = (eps_ref if c == 6 else fo_ref)[at_z : at_z + 8, :]
        own[k * 8 : k * 8 + 8, :] = value
        tiles_y.append(value)
    col_s[0:8, :] = packed(tiles_y, True)
    col_s[8:16, :] = packed(tiles_y, False)

    def rows_at(ref, c, r):
        return ref[pl.ds(c * ROWS + r, NZ, stride=8), :]

    def e_rows(ref, k):
        es[k, 0:NZ, :] = rows_at(ref, 1, 0)
        es[k, NZ : 2 * NZ, :] = rows_at(ref, 2, 0)

    states = (fo_ref, ao_ref)
    pending = {}

    def send_e(k):
        pending[k] = [send(es.at[k], er.at[k], k * 6, dev(-1, 0))]

    e_rows(fo_ref, 0)
    pl.semaphore_wait(barrier, len(peers) + n_gy - 1)

    base = 24
    a_copies = [
        send(up_s, up_r, base + 0, dev(-1, 0)),
        send(down_s, down_r, base + 1, dev(1, 0)),
        send(col_s.at[0:8], col_r.at[0:8], base + 2, dev(0, -1)),
        send(col_s.at[8:16], col_r.at[8:16], base + 3, dev(0, 1)),
        send(cor_s.at[0:8], cor_r.at[0:8], base + 4, dev(-1, -1)),
        send(cor_s.at[8:16], cor_r.at[8:16], base + 5, dev(-1, 1)),
        send(cor_s.at[16:24], cor_r.at[16:24], base + 6, dev(1, -1)),
        send(cor_s.at[24:32], cor_r.at[24:32], base + 7, dev(1, 1)),
    ]
    send_e(0)
    load_a.wait()
    e_rows(ao_ref, 1)
    send_e(1)

    def at(ref, c, b, j):
        return ref[pl.ds(pl.multiple_of(c * ROWS + b * (8 * ZB) + j * 8, 8), 8), :]

    def put(ref, c, b, j, value):
        ref[pl.ds(pl.multiple_of(c * ROWS + b * (8 * ZB) + j * 8, 8), 8), :] = value

    def magnetic_half(s, k):
        ref = states[s]

        def body(b, accs):
            ex = [at(ref, 0, b, j) for j in range(ZB + 1)]
            ey = [at(ref, 1, b, j) for j in range(ZB + 1)]
            ez = [at(ref, 2, b, j) for j in range(ZB)]
            old = [[at(ref, c, b, j) for j in range(ZB)] for c in (3, 4, 5)]
            ex[ZB] = jnp.where(b < NB - 1, ex[ZB], 0.0)
            ey[ZB] = jnp.where(b < NB - 1, ey[ZB], 0.0)

            def along_y(value):
                return jnp.where(lane == 127, 0.0, pltpu.roll(value, 127, 1)) - value

            def along_x(value):
                return jnp.where(row == 7, 0.0, pltpu.roll(value, 7, 0)) - value

            news = [zero, zero]
            made = []
            for j in range(ZB):
                hx = old[0][j] - TIME_STEP * (along_y(ez[j]) - (ey[j + 1] - ey[j]))
                hy = old[1][j] - TIME_STEP * ((ex[j + 1] - ex[j]) - along_x(ez[j]))
                hz = old[2][j] - TIME_STEP * (along_x(ey[j]) - along_y(ex[j]))
                made.append((hx, hy, hz))
                for n, (h, e) in enumerate(((hx, ex[j]), (hz, ez[j]))):
                    both = pltpu.roll(jnp.where(lane == 127, h, e), 2 * j + 1, 1)
                    news[n] = jnp.where((lane >> 1) == j, both, news[n])
            for j in range(ZB):
                for n in range(3):
                    put(ref, 3 + n, b, j, made[j][n])
            return tuple(
                jnp.where(lane // (2 * ZB) == b, pltpu.roll(new, b * (2 * ZB), 1), acc)
                for acc, new in zip(accs, news)
            )

        low, high = lax.fori_loop(0, NB, body, (zero, zero))
        ys[k, 0:8, :] = low
        ys[k, 8:16, :] = high
        hs[k, 0:NZ, :] = rows_at(ref, 4, 7)
        hs[k, NZ : 2 * NZ, :] = rows_at(ref, 5, 7)
        corner = zero
        for m in range(NZ // 8):
            piece = ref[pl.ds(m * 64 + 7, 8, stride=8), :]
            corner = jnp.where(lane == m, pltpu.roll(piece, m, 1) if m else piece, corner)
        cxs[k] = corner
        corner = zero
        for m in range(NZ // 8):
            piece = jnp.broadcast_to(es[k, m * 8 : m * 8 + 8, 127:128], (8, 128))
            corner = jnp.where(lane == 16 * m + 2 * row + 1, piece, corner)
        cys[k] = jnp.broadcast_to(jnp.sum(corner, axis=0, keepdims=True), (8, 128))
        pending[k] += [
            send(hs.at[k], hr.at[k], k * 6 + 1, dev(1, 0)),
            send(ys.at[k], yr_up.at[k], k * 6 + 2, dev(0, -1)),
            send(ys.at[k], yr_down.at[k], k * 6 + 3, dev(0, 1)),
            send(cxs.at[k], cxr.at[k], k * 6 + 4, dev(1, -1)),
            send(cys.at[k], cyr.at[k], k * 6 + 5, dev(-1, 1)),
        ]

    has_next_x = jnp.where(gx < n_gx - 1, 1.0, 0.0)
    has_previous_x = jnp.where(gx > 0, 1.0, 0.0)
    has_next_y = jnp.where(gy < n_gy - 1, 1.0, 0.0)
    has_previous_y = jnp.where(gy > 0, 1.0, 0.0)

    def add_rows(ref, c, value):
        ref[pl.ds(c * ROWS + 7, NZ, stride=8), :] = rows_at(ref, c, 7) + value

    def borders(s, k):
        ref = states[s]
        for copy in pending[k]:
            copy.wait_recv()
        add_rows(ref, 4, er[k, NZ : 2 * NZ, :] * (TIME_STEP * has_next_x))
        add_rows(ref, 5, er[k, 0:NZ, :] * (-TIME_STEP * has_next_x))
        hrow[k, 0:NZ, :] = (hr[k, 0:NZ, :] + TIME_STEP * es[k, NZ : 2 * NZ, :]) * has_previous_x
        for m in range(NZ // 8):
            o = m * 8
            side = jnp.where(lane == 127, pltpu.roll(cxr[k], 127 - m, 1), 0.0) * (TIME_STEP * has_next_y)
            hrow[k, NZ + o : NZ + o + 8, :] = (
                hr[k, NZ + o : NZ + o + 8, :] - TIME_STEP * es[k, o : o + 8, :] + side
            ) * has_previous_x
        corner = jnp.where(row == 7, cyr[k], 0.0) * (TIME_STEP * has_next_x)
        even = (lane & 1) == 0
        return [
            jnp.where(
                even,
                pltpu.roll(up_e, 127, 1) * (factor * has_next_y),
                (down_h + factor * own_e - other) * has_previous_y,
            )
            for up_e, down_h, own_e, factor, other in (
                (yr_up[k, 8:16, :], pltpu.roll(yr_down[k, 0:8, :], 1, 1), ys[k, 8:16, :], -TIME_STEP, zero),
                (yr_up[k, 0:8, :], pltpu.roll(yr_down[k, 8:16, :], 1, 1), ys[k, 0:8, :], TIME_STEP, corner),
            )
        ]

    def electric_block(s, k, sides, b):
        ref = states[s]
        moved = [pltpu.roll(side, 128 - b * (2 * ZB), 1) for side in sides]
        hx, hy, hz = ([at(ref, c, b, j) for j in range(-1 if c < 5 else 0, ZB)] for c in (3, 4, 5))
        hx[0] = jnp.where(b > 0, hx[0], 0.0)
        hy[0] = jnp.where(b > 0, hy[0], 0.0)
        old = [[at(ref, c, b, j) for c in range(3)] for j in range(ZB)]
        us = [at(scale, 0, b, j) for j in range(ZB)]
        behind_hx, behind_hz = [], []
        for j in range(ZB):
            for n, values, o, out in ((0, hx, j + 1, behind_hx), (1, hz, j, behind_hz)):
                side = pltpu.roll(moved[n], 127 - 2 * j, 1)
                values[o] = values[o] + jnp.where(lane == 127, side, 0.0)
                out.append(values[o] - jnp.where(lane == 0, side, pltpu.roll(values[o], 1, 1)))
        new = []
        for j in range(ZB):

            def along_x(value, n, j=j):
                side = wide(hrow[k, pl.ds(n * NZ + b * ZB + j, 1), :])
                return value - jnp.where(row == 0, side, pltpu.roll(value, 1, 0))

            new.append(
                (
                    old[j][0] + us[j] * (behind_hz[j] - (hy[j + 1] - hy[j])),
                    old[j][1] + us[j] * ((hx[j + 1] - hx[j]) - along_x(hz[j], 1)),
                    old[j][2] + us[j] * (along_x(hy[j + 1], 0) - behind_hx[j]),
                )
            )
        for j in range(ZB):
            for n in range(3):
                put(ref, n, b, j, new[j][n])
            put(ref, 3, b, j, hx[j + 1])
            put(ref, 5, b, j, hz[j])
        return old, new

    def electric_step(s, k):
        sides = borders(s, k)

        def body(b, carry):
            electric_block(s, k, sides, b)
            return carry

        lax.fori_loop(0, NB, body, 0)
        e_rows(states[s], k + 2)
        send_e(k + 2)

    def last_step():
        sides = [borders(s, 2 + s) for s in range(2)]
        (a1, b1), (a2, b2) = weights_at(1), weights_at(2)
        k11, k12, k22 = (OMEGA**2 * k for k in (a1 * a1 - b1 * b1, a1 * a2 - b1 * b2, a2 * a2 - b2 * b2))

        def body(b, carry):
            f_old, f_new = electric_block(0, 2, sides[0], b)
            first = [[k11 * p + k12 * q for p, q in zip(*pair)] for pair in zip(f_old, f_new)]
            second = [[k12 * p + k22 * q for p, q in zip(*pair)] for pair in zip(f_old, f_new)]
            a_old, a_new = electric_block(1, 3, sides[1], b)
            for j in range(ZB):
                terms = [a_old[j][n] * first[j][n] + a_new[j][n] * second[j][n] for n in range(3)]
                put(sens_ref, 0, b, j, terms[0] + terms[1] + terms[2])
            return carry

        lax.fori_loop(0, NB, body, 0)

    for s in range(2):
        magnetic_half(s, s)

    def scales(b, carry):
        rows = pl.ds(pl.multiple_of(b * 64, 64), 64)
        scale[rows, :] = 0.5 / eps_ref[rows, :]
        return carry

    lax.fori_loop(0, ROWS // 64, scales, 0)

    for copy in a_copies:
        copy.wait_recv()

    for k in range(len(ROWS_UP)):
        dup[k * 8 : k * 8 + 8, :] = unpacked(cor_r[0:8, :], cor_r[8:16, :], k)
    for k in range(len(ROWS_DOWN)):
        ddown[k * 8 : k * 8 + 8, :] = unpacked(cor_r[16:24, :], cor_r[24:32, :], k)

    far_row = gx * 8 + jnp.where(row < 4, row + 8, row - 8)
    far_lane = gy * 128 + jnp.where(lane < 64, lane + 128, lane - 128)
    row_in = (far_row >= 0) & (far_row < n_gx * 8)
    lane_in = (far_lane >= 0) & (far_lane < n_gy * 128)
    inside = [[None, lane_in], [row_in, row_in & lane_in]]
    where_up = {key: k for k, key in enumerate(ROWS_UP)}
    where_down = {key: k for k, key in enumerate(ROWS_DOWN)}

    def border_rows(up, down, c, z):
        o = z - Z0

        def get(ref, k):
            return wide(ref[k * 8 + o : k * 8 + o + 1, :])

        up0, down0 = get(up, where_up[(c, 0)]), get(down, where_down[(c, 7)])
        out = jnp.where(row < 4, up0, down0)
        if (c, 1) in where_up:
            out = jnp.where(row == 1, get(up, where_up[(c, 1)]), out)
        if (c, 6) in where_down:
            out = jnp.where(row == 6, get(down, where_down[(c, 6)]), out)
        return out

    def masked(q, other=0.0):
        return [
            [q[r][n] if inside[r][n] is None else jnp.where(inside[r][n], q[r][n], other) for n in range(2)]
            for r in range(2)
        ]

    def extended(c, z):
        k = TILES_Y.index((c, z))
        q = [
            [own[k * 8 : k * 8 + 8, :], unpacked(col_r[0:8, :], col_r[8:16, :], k)],
            [border_rows(up_r, down_r, c, z), border_rows(dup, ddown, c, z)],
        ]
        return masked(q, 1.0 if c == 6 else 0.0)

    def combine(fn, *qs):
        return [[fn(*[q[r][n] for q in qs]) for n in range(2)] for r in range(2)]

    def turn_x(q, shift, edge):
        out = [[None, None], [None, None]]
        for n in range(2):
            first, second = pltpu.roll(q[0][n], shift, 0), pltpu.roll(q[1][n], shift, 0)
            out[0][n] = jnp.where(row == edge, second, first)
            out[1][n] = jnp.where(row == edge, first, second)
        return out

    def turn_y(q, shift, edge):
        out = []
        for r in range(2):
            first, second = pltpu.roll(q[r][0], shift, 1), pltpu.roll(q[r][1], shift, 1)
            out.append([jnp.where(lane == edge, second, first), jnp.where(lane == edge, first, second)])
        return out

    def ahead_x(q):
        return combine(jnp.subtract, turn_x(q, 7, 7), q)

    def ahead_y(q):
        return combine(jnp.subtract, turn_y(q, 127, 127), q)

    def behind_x(q):
        return combine(jnp.subtract, q, turn_x(q, 1, 0))

    def behind_y(q):
        return combine(jnp.subtract, q, turn_y(q, 1, 0))

    def half(h, one, two):
        return masked(combine(lambda h, p, q: h - TIME_STEP * (p - q), h, one, two))

    def full(e, us, one, two):
        return masked(combine(lambda e, us, p, q: e + us * (p - q), e, us, one, two))

    def minus(p, q):
        return combine(jnp.subtract, p, q)

    def magnetic(e, h, zs):
        for z in zs:
            ex, ey, ez = (e[(c, z)] for c in range(3))
            h[(3, z)] = half(h[(3, z)], ahead_y(ez), minus(e[(1, z + 1)], ey))
            h[(4, z)] = half(h[(4, z)], minus(e[(0, z + 1)], ex), ahead_x(ez))
            h[(5, z)] = half(h[(5, z)], ahead_x(ey), ahead_y(ex))

    e = {(c, z): extended(c, z) for c, z in TILES_Y if c < 3}
    h = {(c, z): extended(c, z) for c, z in TILES_Y if 3 <= c < 6}
    us = {z: combine(lambda p: 0.5 / p, extended(6, z)) for c, z in TILES_Y if c == 6}
    magnetic(e, h, range(Z0, Z0 + 4))
    h1 = [h[(3, ZM)][0][0], h[(4, ZM)][0][0]]
    for z in range(Z0 + 1, Z0 + 4):
        hx, hy, hz = (h[(c, z)] for c in (3, 4, 5))
        e[(0, z)] = full(e[(0, z)], us[z], behind_y(hz), minus(hy, h[(4, z - 1)]))
        e[(1, z)] = full(e[(1, z)], us[z], minus(hx, h[(3, z - 1)]), behind_x(hz))
        e[(2, z)] = full(e[(2, z)], us[z], behind_x(hy), behind_y(hx))
    e1 = [e[(0, ZM)][0][0], e[(1, ZM)][0][0]]
    magnetic(e, h, range(Z0 + 1, Z0 + 3))
    h2 = [h[(3, ZM)][0][0], h[(4, ZM)][0][0]]
    hz = h[(5, ZM)]
    us_m = us[ZM][0][0]
    e2 = [
        e1[0] + us_m * (behind_y(hz)[0][0] - (h2[1] - h[(4, ZM - 1)][0][0])),
        e1[1] + us_m * ((h2[0] - h[(3, ZM - 1)][0][0]) - behind_x(hz)[0][0]),
    ]
    for part_of in range(2):
        first, second = weights_at(0.5)[part_of], weights_at(1.5)[part_of]
        hx, hy = (first * h1[n] + second * h2[n] for n in range(2))
        first, second = weights_at(1)[part_of], weights_at(2)[part_of]
        ex, ey = (first * e1[n] + second * e2[n] for n in range(2))
        for n, value in enumerate((-hy, hx, ey, -ex)):
            gath[0, (part_of * 4 + n) * 8 : (part_of * 4 + n) * 8 + 8, :] = value

    base_g = base + 8
    g_copies = [send(gath.at[0], gath.at[d], base_g + d - 1, zh_peer(d)) for d in range(1, n_zh)]

    for copy in load_rest:
        copy.wait()
    n_w = n_xi * 2 * n_gy
    n_k = n_zh * 16
    wrow = iota((n_w, 128), 0)
    wlane = iota((n_w, 128), 1)
    u = zh * (n_xi * n_gy) + (wrow // (2 * n_gy)) * n_gy + wrow % n_gy
    imag_out = (wrow // n_gy) % 2
    back = wlane // 16
    imag_in = (wlane // 8) % 2
    x = (((zh - back + n_zh) % n_zh) * n_xi + xi) * 8 + wlane % 8
    n_u = n_gx * n_gy
    weights = cos_turns((2 * u + 1 - n_u) * x * (4096 // (16 * n_u)) + 1024 * (imag_out - imag_in))
    hits = jnp.zeros((n_w, 128), F32)
    for d in range(n_zh):
        t = tile_of(d)
        same = (lists_ref[d, pl.ds(t % 8, 1), :] == u[:, : lists_ref.shape[2]]).astype(F32)
        count = jnp.sum(same, axis=1, keepdims=True) * mask_ref[t].astype(F32)
        hits = jnp.where(back == d, count, hits)
    wtab[...] = weights * hits

    def v_rows(b, carry):
        y = b * 8 + iota((8, 512), 0)
        v = iota((8, 512), 1)
        vtab[pl.ds(pl.multiple_of(b * 8, 8), 8), :] = cos_turns(
            (2 * (v & 255) - 255) * y - 1024 * (v >> 8)
        )
        return carry

    lax.fori_loop(0, 16, v_rows, 0)
    d = iota((n_gy, 512), 0)
    v = iota((n_gy, 512), 1)
    tws[...] = cos_turns((2 * (v & 255) - 255) * (((gy - d + n_gy) % n_gy) * 128) - 1024 * (v >> 8))

    electric_step(0, 0)
    magnetic_half(0, 2)

    for copy in g_copies:
        copy.wait_recv()
    table = wtab[:, 0:n_k]
    blk = 8 * n_gy
    for c in range(4):
        planes = jnp.concatenate(
            [gath[d, (4 * r + c) * 8 : (4 * r + c) * 8 + 8, :] for d in range(n_zh) for r in range(2)], axis=0
        )
        out = jnp.dot(table, planes, preferred_element_type=F32, precision=HIGHEST)
        for q in range(n_xi):
            for r in range(2):
                part[q * blk + r * 4 * n_gy + c * n_gy : q * blk + r * 4 * n_gy + (c + 1) * n_gy, :] = out[
                    (q * 2 + r) * n_gy : (q * 2 + r + 1) * n_gy, :
                ]
    base_r = base_g + n_zh - 1
    r_copies = []
    for d in range(1, n_xi):
        to = (xi + d) % n_xi
        r_copies.append(
            send(
                part.at[pl.ds(pl.multiple_of(to * blk, blk), blk)], part_r.at[d - 1], base_r + d - 1, xi_peer(d)
            )
        )

    electric_step(1, 1)
    magnetic_half(1, 3)

    for copy in r_copies:
        copy.wait_recv()
    acc = part[pl.ds(pl.multiple_of(xi * blk, blk), blk), :]
    for d in range(1, n_xi):
        acc = acc + part_r[d - 1]
    total[...] = acc
    for j in range(n_gy):
        rows_s[j] = total[pl.ds(j, 8, stride=n_gy), :]
    rows_r[0] = rows_s[gy]
    base_a = base_r + n_xi - 1
    last_copies = []
    for d in range(1, n_gy):
        to = (gy + d) % n_gy
        last_copies.append(
            send(rows_s.at[to], rows_r.at[d], base_a + d - 1, {"gx": gx, "gy": to})
        )

    last_step()

    for copy in last_copies:
        copy.wait_recv()
    turned = jnp.dot(
        rows_r[...].reshape(n_gy * 8, 128), vtab[...], preferred_element_type=F32, precision=HIGHEST
    )
    sign = jnp.where(iota((8, 256), 0) < 4, 1.0, -1.0)
    out = jnp.zeros((8, 256), F32)
    for d in range(n_gy):
        rows = turned[d * 8 : d * 8 + 8, :]
        value = rows[:, :256] + sign * pltpu.roll(rows[:, 256:], 4, 0)
        out = out + tws[d : d + 1, :256] * value + tws[d : d + 1, 256:] * (sign * pltpu.roll(value, 4, 0))
    far_ref[...] = out * (1.0 / math.sqrt(CX * CY))

    for copy in started:
        copy.wait_send()


def write_out(*refs):
    n = len(refs) // 2
    sems = refs[-1]
    copies = [pltpu.make_async_copy(refs[i], refs[n + i], sems.at[i]) for i in range(n)]
    for copy in copies:
        copy.start()
    for copy in copies:
        copy.wait()


def solution(mesh):
    n_gx, n_gy = mesh.shape["gx"], mesh.shape["gy"]
    n_xi = 4 if n_gx == 16 else n_gx
    dims = (n_gx // n_xi, n_xi, n_gy)
    n_zh = dims[0]
    n_sem = 24 + 8 + (n_zh - 1) + (n_xi - 1) + (n_gy - 1)
    vmem = pl.BlockSpec(memory_space=pltpu.VMEM)
    hbm = pl.BlockSpec(memory_space=pltpu.HBM)
    blk = 8 * n_gy

    def buffer(*shape):
        return pltpu.VMEM(shape, F32)

    def shards(fields, adjoint, permittivity, lists, mask):
        shapes = (
            jax.ShapeDtypeStruct((6 * ROWS, 128), F32),
            jax.ShapeDtypeStruct((6 * ROWS, 128), F32),
            jax.ShapeDtypeStruct((ROWS, 128), F32),
            jax.ShapeDtypeStruct((8, 256), F32),
        )
        made = pl.pallas_call(
            functools.partial(kernel, dims),
            out_shape=shapes,
            in_specs=[hbm] * 5,
            out_specs=(vmem,) * 4,
            scratch_shapes=[
                buffer(ROWS, 128),
                pltpu.VMEM((n_zh, 8, lists.shape[1]), jnp.int32),
                pltpu.SMEM(mask.shape, jnp.int32),
                buffer(ROWS, 128),
                buffer(8 * len(TILES_Y), 128),
                buffer(4, 2 * NZ, 128), buffer(4, 2 * NZ, 128), buffer(4, 2 * NZ, 128), buffer(4, 2 * NZ, 128),
                buffer(4, 16, 128), buffer(4, 16, 128), buffer(4, 16, 128),
                buffer(4, 8, 128), buffer(4, 8, 128), buffer(4, 8, 128), buffer(4, 8, 128),
                buffer(4, 2 * NZ, 128),
                buffer(72, 128), buffer(96, 128), buffer(16, 128), buffer(32, 128),
                buffer(72, 128), buffer(96, 128), buffer(16, 128), buffer(32, 128),
                buffer(72, 128), buffer(96, 128),
                buffer(n_zh, 64, 128), buffer(n_xi * 2 * n_gy, 128), buffer(128, 512), buffer(n_gy, 512),
                buffer(n_xi * blk, 128), buffer(max(n_xi - 1, 1), blk, 128), buffer(blk, 128),
                buffer(n_gy, 8, 128), buffer(n_gy, 8, 128),
                pltpu.SemaphoreType.DMA((4 + n_zh,)),
                pltpu.SemaphoreType.DMA((n_sem,)),
                pltpu.SemaphoreType.DMA((n_sem,)),
            ],
            compiler_params=pltpu.CompilerParams(
                collective_id=0, has_side_effects=True, vmem_limit_bytes=58 * 1024 * 1024
            ),
        )(
            fields.reshape(6 * ROWS, 128),
            adjoint.reshape(6 * ROWS, 128),
            permittivity.reshape(ROWS, 128),
            lists,
            mask,
        )
        out = pl.pallas_call(
            write_out,
            out_shape=shapes,
            in_specs=[vmem] * 4,
            out_specs=(pl.BlockSpec(memory_space=pl.ANY),) * 4,
            scratch_shapes=[pltpu.SemaphoreType.DMA((4,))],
        )(*made)
        return (
            out[0].reshape(fields.shape),
            out[1].reshape(fields.shape),
            out[2].reshape(permittivity.shape),
            out[3].reshape(1, 8, 256),
        )

    in_specs = (P(None, None, "gx", "gy"), P(None, None, "gx", "gy"), P(None, "gx", "gy"), P(), P())
    out_specs = (
        P(None, None, "gx", "gy"),
        P(None, None, "gx", "gy"),
        P(None, "gx", "gy"),
        P(("gx", "gy"), None, None),
    )
    return jax.shard_map(shards, mesh=mesh, in_specs=in_specs, out_specs=out_specs, check_vma=False)
```

time: 55.4 us -> 41.1 us (0.74)
  the two profiles are of different devices: /device:TPU:32 before, /device:TPU:1 now
where the time goes in v2:
time: 41.1 us; the launch traced here: 40.6 us
  Pallas kernels  40 us (97%)
  between operations  0.64 us (2%)
    pallas_call x1, Pallas kernels, shards(): pl.pallas_call(functools.partial(kernel, dims), out_shape=shapes, in_spec...  36.9 us
    pallas_call x1, Pallas kernels, shards(): pl.pallas_call(write_out, out_shape=shapes, in_specs=[vmem] * 4, out_spec...  3.13 us

profile of v2, /device:TPU:1, one launch (start us, length us, event | category | flops | bytes accessed | tf_op | source)
XLA Modules:
  0.0 40.6 jit_solution(6132543234673045488)
XLA Ops:
  0.6 36.9 %shard_map.84 = (f32[2304,128]{1,0:T(8,128)}, f32[2304,128]{1,0:T(8,128)}, f32[384,128]{1,0:T(8,128)}, f32[8,256]{1,0:T(8,128)}) custom-call(f32[2304,128]{1,0:T(8,128)} %bitcast.7, f32[2304,128]{1,0:T(8,128)} %bitcast.8, f32[384,128]{1,0:T(8,128)} %bitcast.9, s32[256,128]{1,0:T(8,128)} %lists_hbm.1, s32[256]{0:T(256)} %mask_hbm.1), custom_call_target="tpu_custom_call" | custom-call | tf_op jit(solution)/shard_map/pallas_call | solution.py:621
  37.5 3.1 %shard_map.85 = (f32[2304,128]{1,0:T(8,128)}, f32[2304,128]{1,0:T(8,128)}, f32[384,128]{1,0:T(8,128)}, f32[8,256]{1,0:T(8,128)}) custom-call(f32[2304,128]{1,0:T(8,128)} %get-tuple-element.12.refs_0_, f32[2304,128]{1,0:T(8,128)} %get-tuple-element.13.refs_1_, f32[384,128]{1,0:T(8,128)} %get-tuple-element.14.refs_2_, f32[8,256]{1,0:T(8,128)} %get-tuple-element.15.refs_3_), custom_call_target="tpu_custom_call" | custom-call | tf_op jit(solution)/shard_map/pallas_call | solution.py:656

commit v3 on v2

--- a/solution.py
+++ b/solution.py
@@ -18,7 +18,7 @@
 HIGHEST = lax.Precision.HIGHEST
 MESH = pl.DeviceIdType.MESH
 F32 = jnp.float32
-ZB = 8
+ZB = 24
 NB = NZ // ZB
 
 ROWS_UP = [(c, 0) for c in range(6)] + [(1, 1), (2, 1), (6, 0)]
@@ -362,11 +362,11 @@
         magnetic_half(s, s)
 
     def scales(b, carry):
-        rows = pl.ds(pl.multiple_of(b * 64, 64), 64)
+        rows = pl.ds(pl.multiple_of(b * 192, 192), 192)
         scale[rows, :] = 0.5 / eps_ref[rows, :]
         return carry
 
-    lax.fori_loop(0, ROWS // 64, scales, 0)
+    lax.fori_loop(0, ROWS // 192, scales, 0)
 
     for copy in a_copies:
         copy.wait_recv()
@@ -510,14 +510,14 @@
     wtab[...] = weights * hits
 
     def v_rows(b, carry):
-        y = b * 8 + iota((8, 512), 0)
-        v = iota((8, 512), 1)
-        vtab[pl.ds(pl.multiple_of(b * 8, 8), 8), :] = cos_turns(
+        y = b * 32 + iota((32, 512), 0)
+        v = iota((32, 512), 1)
+        vtab[pl.ds(pl.multiple_of(b * 32, 32), 32), :] = cos_turns(
             (2 * (v & 255) - 255) * y - 1024 * (v >> 8)
         )
         return carry
 
-    lax.fori_loop(0, 16, v_rows, 0)
+    lax.fori_loop(0, 4, v_rows, 0)
     d = iota((n_gy, 512), 0)
     v = iota((n_gy, 512), 1)
     tws[...] = cos_turns((2 * (v & 255) - 255) * (((gy - d + n_gy) % n_gy) * 128) - 1024 * (v >> 8))
@@ -620,7 +620,7 @@
         )
         made = pl.pallas_call(
             functools.partial(kernel, dims),
-            out_shape=shapes,
+            out_shape=tuple(pltpu.VMEM(shape.shape, F32) for shape in shapes),
             in_specs=[hbm] * 5,
             out_specs=(vmem,) * 4,
             scratch_shapes=[
@@ -644,21 +644,27 @@
                 pltpu.SemaphoreType.DMA((n_sem,)),
             ],
             compiler_params=pltpu.CompilerParams(
-                collective_id=0, has_side_effects=True, vmem_limit_bytes=58 * 1024 * 1024
+                collective_id=0, has_side_effects=True, vmem_limit_bytes=40 * 1024 * 1024
             ),
         )(
-            fields.reshape(6 * ROWS, 128),
-            adjoint.reshape(6 * ROWS, 128),
-            permittivity.reshape(ROWS, 128),
-            lists,
-            mask,
+            *[
+                pltpu.with_memory_space_constraint(value, pltpu.HBM)
+                for value in (
+                    fields.reshape(6 * ROWS, 128),
+                    adjoint.reshape(6 * ROWS, 128),
+                    permittivity.reshape(ROWS, 128),
+                    lists,
+                    mask,
+                )
+            ]
         )
         out = pl.pallas_call(
             write_out,
             out_shape=shapes,
-            in_specs=[vmem] * 4,
+            in_specs=[pl.BlockSpec(memory_space=pl.ANY)] * 4,
             out_specs=(pl.BlockSpec(memory_space=pl.ANY),) * 4,
             scratch_shapes=[pltpu.SemaphoreType.DMA((4,))],
+            compiler_params=pltpu.CompilerParams(vmem_limit_bytes=1024 * 1024),
         )(*made)
         return (
             out[0].reshape(fields.shape),

time: 41.1 us -> 37.4 us (0.910)
  Pallas kernels: 40 us -> 36.6 us
    pallas_call x2, Pallas kernels: 40 us -> 36.6 us  [the longest x1 35.1 us: shards(): pl.pallas_call(functools.partial(kernel, dims), out_shape=tuple((pltpu.VM...]
where the time goes in v3:
time: 37.4 us; the launch traced here: 37.3 us
  Pallas kernels  36.6 us (98%)
  between operations  0.64 us (2%)
    pallas_call x1, Pallas kernels, shards(): pl.pallas_call(functools.partial(kernel, dims), out_shape=tuple((pltpu.VM...  35.1 us
    pallas_call x1, Pallas kernels, shards(): pl.pallas_call(write_out, out_shape=shapes, in_specs=[pl.BlockSpec(memory...  1.49 us

profile of v3, /device:TPU:1, one launch (start us, length us, event | category | flops | bytes accessed | tf_op | source)
XLA Modules:
  0.0 37.3 jit_solution(6265156098326508621)
XLA Ops:
  0.6 35.1 %shard_map.84 = (f32[2304,128]{1,0:T(8,128)S(1)}, f32[2304,128]{1,0:T(8,128)S(1)}, f32[384,128]{1,0:T(8,128)S(1)}, f32[8,256]{1,0:T(8,128)S(1)}) custom-call(f32[2304,128]{1,0:T(8,128)} %bitcast.7, f32[2304,128]{1,0:T(8,128)} %bitcast.8, f32[384,128]{1,0:T(8,128)} %bitcast.9, s32[256,128]{1,0:T(8,128)} %lists_hbm.1, s32[256]{0:T(256)} %mask_hbm.1), custom_call_target="tpu_custom_call" | custom-call | tf_op jit(solution)/shard_map/pallas_call | solution.py:621
  35.8 1.5 %shard_map.85 = (f32[2304,128]{1,0:T(8,128)}, f32[2304,128]{1,0:T(8,128)}, f32[384,128]{1,0:T(8,128)}, f32[8,256]{1,0:T(8,128)}) custom-call(f32[2304,128]{1,0:T(8,128)S(1)} %get-tuple-element.12.refs_0_, f32[2304,128]{1,0:T(8,128)S(1)} %get-tuple-element.13.refs_1_, f32[384,128]{1,0:T(8,128)S(1)} %get-tuple-element.14.refs_2_, ...), custom_call_target="tpu_custom_call" | custom-call | tf_op jit(solution)/shard_map/pallas_call | solution.py:661

commit v4 on v3

--- a/solution.py
+++ b/solution.py
@@ -15,14 +15,16 @@
 TIME_STEP = 0.5
 PHASE_STEP = 0.3
 OMEGA = PHASE_STEP / TIME_STEP
-HIGHEST = lax.Precision.HIGHEST
 MESH = pl.DeviceIdType.MESH
 F32 = jnp.float32
 ZB = 24
 NB = NZ // ZB
 
-ROWS_UP = [(c, 0) for c in range(6)] + [(1, 1), (2, 1), (6, 0)]
-ROWS_DOWN = [(c, 7) for c in range(6)] + [(c, 6) for c in (0, 1, 2, 4, 5)] + [(6, 7)]
+ROWS_UP = [((0, 0), (6, 0)), ((1, 0),), ((2, 0),), ((3, 0), (4, 0)), ((5, 0), (1, 1)), ((2, 1),)]
+ROWS_DOWN = [
+    ((0, 7), (6, 7)), ((1, 7),), ((2, 7),), ((3, 7), (4, 7)), ((5, 7), (4, 6)), ((0, 6),), ((1, 6), (2, 6)), ((5, 6),)
+]
+N_UP, N_DOWN = len(ROWS_UP), len(ROWS_DOWN)
 TILES_Y = (
     [(c, z) for c in range(3) for z in range(Z0, Z0 + 5)]
     + [(c, z) for c in range(3, 6) for z in range(Z0, Z0 + 4)]
@@ -46,6 +48,18 @@
     return jnp.where(((quarter + 1) & 2) == 2, -value, value)
 
 
+def halves(value):
+    high = value.astype(jnp.bfloat16)
+    return high, (value - high.astype(F32)).astype(jnp.bfloat16)
+
+
+def product(left, right):
+    return (
+        jnp.dot(left[0], right[1], preferred_element_type=F32)
+        + jnp.dot(left[1], right[0], preferred_element_type=F32)
+    ) + jnp.dot(left[0], right[0], preferred_element_type=F32)
+
+
 def iota(shape, axis):
     return lax.broadcasted_iota(jnp.int32, shape, axis)
 
@@ -58,7 +72,7 @@
     dims,
     f_hbm, a_hbm, eps_hbm, lists_hbm, mask_hbm,
     fo_ref, ao_ref, sens_ref, far_ref,
-    eps_ref, lists_ref, mask_ref, scale, own,
+    eps_ref, lists_ref, mask_ref, scale, slab, mixed,
     es, er, hs, hr, ys, yr_up, yr_down, cxs, cxr, cys, cyr, hrow,
     up_s, down_s, col_s, cor_s, up_r, down_r, col_r, cor_r, dup, ddown,
     gath, wtab, vtab, tws, part, part_r, total, rows_s, rows_r,
@@ -80,6 +94,25 @@
     def xi_peer(d):
         return {"gx": zh * n_xi + (xi + d) % n_xi, "gy": gy}
 
+    def load(src, dst, slot):
+        copy = pltpu.make_async_copy(src, dst, load_sem.at[slot])
+        copy.start()
+        return copy
+
+    def tile_of(d):
+        return (((zh - d + n_zh) % n_zh) * n_xi + xi) * n_gy + gy
+
+    load_slab = [
+        load(f_hbm.at[pl.ds(c * ROWS + Z0 * 8, 64)], slab.at[pl.ds(c * 64, 64)], 4 + n_zh + c) for c in range(6)
+    ]
+    load_eps = load(eps_hbm, eps_ref, 1)
+    load_f = load(f_hbm, fo_ref, 0)
+    load_a = load(a_hbm, ao_ref, 2)
+    load_rest = [load(mask_hbm, mask_ref, 3)]
+    for d in range(n_zh):
+        first = pl.multiple_of(tile_of(d) // 8 * 8, 8)
+        load_rest.append(load(lists_hbm.at[pl.ds(first, 8)], lists_ref.at[d], 4 + d))
+
     barrier = pltpu.get_barrier_semaphore()
     peers = [dev(dx, dy) for dx in (-1, 1) for dy in (-1, 0, 1)]
     peers += [zh_peer(d) for d in range(1, n_zh)] + [xi_peer(d) for d in range(1, n_xi)]
@@ -93,22 +126,6 @@
         return carry
 
     lax.fori_loop(1, n_gy, greet, 0)
-
-    def load(src, dst, slot):
-        copy = pltpu.make_async_copy(src, dst, load_sem.at[slot])
-        copy.start()
-        return copy
-
-    def tile_of(d):
-        return (((zh - d + n_zh) % n_zh) * n_xi + xi) * n_gy + gy
-
-    load_f = load(f_hbm, fo_ref, 0)
-    load_eps = load(eps_hbm, eps_ref, 1)
-    load_a = load(a_hbm, ao_ref, 2)
-    load_rest = [load(mask_hbm, mask_ref, 3)]
-    for d in range(n_zh):
-        first = pl.multiple_of(tile_of(d) // 8 * 8, 8)
-        load_rest.append(load(lists_hbm.at[pl.ds(first, 8)], lists_ref.at[d], 4 + d))
 
     started = []
 
@@ -128,7 +145,7 @@
     def layer(c, r):
         if c == 6:
             return eps_ref[pl.ds(Z0 * 8 + r, 8, stride=8), :]
-        return fo_ref[pl.ds(c * ROWS + Z0 * 8 + r, 8, stride=8), :]
+        return slab[pl.ds(c * 64 + r, 8, stride=8), :]
 
     def packed(values, low):
         out = zero
@@ -143,10 +160,17 @@
         second = pltpu.roll(high, (126 - 2 * k) % 128, 1)
         return jnp.where(lane < 64, first, second)
 
-    load_f.wait()
+    for copy in load_slab:
+        copy.wait()
     load_eps.wait()
-    ups = [layer(c, r) for c, r in ROWS_UP]
-    downs = [layer(c, r) for c, r in ROWS_DOWN]
+    def layers(keys):
+        first = layer(*keys[0])
+        if len(keys) == 1:
+            return first
+        return jnp.where(row < (5 if keys[1][0] == 6 else 4), first, pltpu.roll(layer(*keys[1]), 4, 0))
+
+    ups = [layers(keys) for keys in ROWS_UP]
+    downs = [layers(keys) for keys in ROWS_DOWN]
     for k, value in enumerate(ups):
         up_s[k * 8 : k * 8 + 8, :] = value
     for k, value in enumerate(downs):
@@ -155,12 +179,12 @@
     cor_s[8:16, :] = packed(ups, False)
     cor_s[16:24, :] = packed(downs, True)
     cor_s[24:32, :] = packed(downs, False)
-    tiles_y = []
-    for k, (c, z) in enumerate(TILES_Y):
-        at_z = z * 8 if c == 6 else c * ROWS + z * 8
-        value = (eps_ref if c == 6 else fo_ref)[at_z : at_z + 8, :]
-        own[k * 8 : k * 8 + 8, :] = value
-        tiles_y.append(value)
+    def tile(c, z):
+        if c == 6:
+            return eps_ref[z * 8 : z * 8 + 8, :]
+        return slab[c * 64 + (z - Z0) * 8 : c * 64 + (z - Z0) * 8 + 8, :]
+
+    tiles_y = [tile(c, z) for c, z in TILES_Y]
     col_s[0:8, :] = packed(tiles_y, True)
     col_s[8:16, :] = packed(tiles_y, False)
 
@@ -177,7 +201,6 @@
     def send_e(k):
         pending[k] = [send(es.at[k], er.at[k], k * 6, dev(-1, 0))]
 
-    e_rows(fo_ref, 0)
     pl.semaphore_wait(barrier, len(peers) + n_gy - 1)
 
     base = 24
@@ -191,6 +214,8 @@
         send(cor_s.at[16:24], cor_r.at[16:24], base + 6, dev(1, -1)),
         send(cor_s.at[24:32], cor_r.at[24:32], base + 7, dev(1, 1)),
     ]
+    load_f.wait()
+    e_rows(fo_ref, 0)
     send_e(0)
     load_a.wait()
     e_rows(ao_ref, 1)
@@ -341,18 +366,29 @@
         e_rows(states[s], k + 2)
         send_e(k + 2)
 
-    def last_step():
-        sides = [borders(s, 2 + s) for s in range(2)]
-        (a1, b1), (a2, b2) = weights_at(1), weights_at(2)
-        k11, k12, k22 = (OMEGA**2 * k for k in (a1 * a1 - b1 * b1, a1 * a2 - b1 * b2, a2 * a2 - b2 * b2))
+    (a1, b1), (a2, b2) = weights_at(1), weights_at(2)
+    k11, k12, k22 = (OMEGA**2 * k for k in (a1 * a1 - b1 * b1, a1 * a2 - b1 * b2, a2 * a2 - b2 * b2))
+
+    def last_forward():
+        sides = borders(0, 2)
 
         def body(b, carry):
-            f_old, f_new = electric_block(0, 2, sides[0], b)
-            first = [[k11 * p + k12 * q for p, q in zip(*pair)] for pair in zip(f_old, f_new)]
-            second = [[k12 * p + k22 * q for p, q in zip(*pair)] for pair in zip(f_old, f_new)]
-            a_old, a_new = electric_block(1, 3, sides[1], b)
+            old, new = electric_block(0, 2, sides, b)
             for j in range(ZB):
-                terms = [a_old[j][n] * first[j][n] + a_new[j][n] * second[j][n] for n in range(3)]
+                for n in range(3):
+                    put(mixed, n, b, j, k11 * old[j][n] + k12 * new[j][n])
+                    put(mixed, 3 + n, b, j, k12 * old[j][n] + k22 * new[j][n])
+            return carry
+
+        lax.fori_loop(0, NB, body, 0)
+
+    def last_adjoint():
+        sides = borders(1, 3)
+
+        def body(b, carry):
+            old, new = electric_block(1, 3, sides, b)
+            for j in range(ZB):
+                terms = [old[j][n] * at(mixed, n, b, j) + new[j][n] * at(mixed, 3 + n, b, j) for n in range(3)]
                 put(sens_ref, 0, b, j, terms[0] + terms[1] + terms[2])
             return carry
 
@@ -381,14 +417,17 @@
     row_in = (far_row >= 0) & (far_row < n_gx * 8)
     lane_in = (far_lane >= 0) & (far_lane < n_gy * 128)
     inside = [[None, lane_in], [row_in, row_in & lane_in]]
-    where_up = {key: k for k, key in enumerate(ROWS_UP)}
-    where_down = {key: k for k, key in enumerate(ROWS_DOWN)}
+    where_up, where_down = (
+        {key: 8 * k + 4 * n for k, keys in enumerate(table) for n, key in enumerate(keys)}
+        for table in (ROWS_UP, ROWS_DOWN)
+    )
 
     def border_rows(up, down, c, z):
         o = z - Z0
 
-        def get(ref, k):
-            return wide(ref[k * 8 + o : k * 8 + o + 1, :])
+        def get(ref, start):
+            at_z = start + (o if start % 8 + o < 8 else 0)
+            return wide(ref[at_z : at_z + 1, :])
 
         up0, down0 = get(up, where_up[(c, 0)]), get(down, where_down[(c, 7)])
         out = jnp.where(row < 4, up0, down0)
@@ -407,7 +446,7 @@
     def extended(c, z):
         k = TILES_Y.index((c, z))
         q = [
-            [own[k * 8 : k * 8 + 8, :], unpacked(col_r[0:8, :], col_r[8:16, :], k)],
+            [tile(c, z), unpacked(col_r[0:8, :], col_r[8:16, :], k)],
             [border_rows(up_r, down_r, c, z), border_rows(dup, ddown, c, z)],
         ]
         return masked(q, 1.0 if c == 6 else 0.0)
@@ -507,14 +546,13 @@
         same = (lists_ref[d, pl.ds(t % 8, 1), :] == u[:, : lists_ref.shape[2]]).astype(F32)
         count = jnp.sum(same, axis=1, keepdims=True) * mask_ref[t].astype(F32)
         hits = jnp.where(back == d, count, hits)
-    wtab[...] = weights * hits
+    wtab[0], wtab[1] = halves(weights * hits)
 
     def v_rows(b, carry):
         y = b * 32 + iota((32, 512), 0)
         v = iota((32, 512), 1)
-        vtab[pl.ds(pl.multiple_of(b * 32, 32), 32), :] = cos_turns(
-            (2 * (v & 255) - 255) * y - 1024 * (v >> 8)
-        )
+        rows = pl.ds(pl.multiple_of(b * 32, 32), 32)
+        vtab[0, rows, :], vtab[1, rows, :] = halves(cos_turns((2 * (v & 255) - 255) * y - 1024 * (v >> 8)))
         return carry
 
     lax.fori_loop(0, 4, v_rows, 0)
@@ -527,13 +565,13 @@
 
     for copy in g_copies:
         copy.wait_recv()
-    table = wtab[:, 0:n_k]
+    table = (wtab[0][:, 0:n_k], wtab[1][:, 0:n_k])
     blk = 8 * n_gy
     for c in range(4):
         planes = jnp.concatenate(
             [gath[d, (4 * r + c) * 8 : (4 * r + c) * 8 + 8, :] for d in range(n_zh) for r in range(2)], axis=0
         )
-        out = jnp.dot(table, planes, preferred_element_type=F32, precision=HIGHEST)
+        out = product(table, halves(planes))
         for q in range(n_xi):
             for r in range(2):
                 part[q * blk + r * 4 * n_gy + c * n_gy : q * blk + r * 4 * n_gy + (c + 1) * n_gy, :] = out[
@@ -569,13 +607,12 @@
             send(rows_s.at[to], rows_r.at[d], base_a + d - 1, {"gx": gx, "gy": to})
         )
 
-    last_step()
+    last_forward()
+    last_adjoint()
 
     for copy in last_copies:
         copy.wait_recv()
-    turned = jnp.dot(
-        rows_r[...].reshape(n_gy * 8, 128), vtab[...], preferred_element_type=F32, precision=HIGHEST
-    )
+    turned = product(halves(rows_r[...].reshape(n_gy * 8, 128)), (vtab[0], vtab[1]))
     sign = jnp.where(iota((8, 256), 0) < 4, 1.0, -1.0)
     out = jnp.zeros((8, 256), F32)
     for d in range(n_gy):
@@ -588,10 +625,17 @@
         copy.wait_send()
 
 
+PIECES = ((0, 4), (1, 4), (2, 1), (3, 1))
+
+
 def write_out(*refs):
-    n = len(refs) // 2
     sems = refs[-1]
-    copies = [pltpu.make_async_copy(refs[i], refs[n + i], sems.at[i]) for i in range(n)]
+    copies = []
+    for i, pieces in PIECES:
+        rows = refs[i].shape[0] // pieces
+        for p in range(pieces):
+            part = pl.ds(p * rows, rows)
+            copies.append(pltpu.make_async_copy(refs[i].at[part], refs[4 + i].at[part], sems.at[len(copies)]))
     for copy in copies:
         copy.start()
     for copy in copies:
@@ -628,18 +672,18 @@
                 pltpu.VMEM((n_zh, 8, lists.shape[1]), jnp.int32),
                 pltpu.SMEM(mask.shape, jnp.int32),
                 buffer(ROWS, 128),
-                buffer(8 * len(TILES_Y), 128),
+                buffer(6 * 64, 128), buffer(6 * ROWS, 128),
                 buffer(4, 2 * NZ, 128), buffer(4, 2 * NZ, 128), buffer(4, 2 * NZ, 128), buffer(4, 2 * NZ, 128),
                 buffer(4, 16, 128), buffer(4, 16, 128), buffer(4, 16, 128),
                 buffer(4, 8, 128), buffer(4, 8, 128), buffer(4, 8, 128), buffer(4, 8, 128),
                 buffer(4, 2 * NZ, 128),
-                buffer(72, 128), buffer(96, 128), buffer(16, 128), buffer(32, 128),
-                buffer(72, 128), buffer(96, 128), buffer(16, 128), buffer(32, 128),
-                buffer(72, 128), buffer(96, 128),
-                buffer(n_zh, 64, 128), buffer(n_xi * 2 * n_gy, 128), buffer(128, 512), buffer(n_gy, 512),
+                buffer(8 * N_UP, 128), buffer(8 * N_DOWN, 128), buffer(16, 128), buffer(32, 128),
+                buffer(8 * N_UP, 128), buffer(8 * N_DOWN, 128), buffer(16, 128), buffer(32, 128),
+                buffer(8 * N_UP, 128), buffer(8 * N_DOWN, 128),
+                buffer(n_zh, 64, 128), pltpu.VMEM((2, n_xi * 2 * n_gy, 128), jnp.bfloat16), pltpu.VMEM((2, 128, 512), jnp.bfloat16), buffer(n_gy, 512),
                 buffer(n_xi * blk, 128), buffer(max(n_xi - 1, 1), blk, 128), buffer(blk, 128),
                 buffer(n_gy, 8, 128), buffer(n_gy, 8, 128),
-                pltpu.SemaphoreType.DMA((4 + n_zh,)),
+                pltpu.SemaphoreType.DMA((4 + n_zh + 6,)),
                 pltpu.SemaphoreType.DMA((n_sem,)),
                 pltpu.SemaphoreType.DMA((n_sem,)),
             ],
@@ -663,7 +707,7 @@
             out_shape=shapes,
             in_specs=[pl.BlockSpec(memory_space=pl.ANY)] * 4,
             out_specs=(pl.BlockSpec(memory_space=pl.ANY),) * 4,
-            scratch_shapes=[pltpu.SemaphoreType.DMA((4,))],
+            scratch_shapes=[pltpu.SemaphoreType.DMA((10,))],
             compiler_params=pltpu.CompilerParams(vmem_limit_bytes=1024 * 1024),
         )(*made)
         return (

time: 37.4 us -> 36.9 us (0.987)
  Pallas kernels: 36.6 us -> 36.1 us
    pallas_call x1, Pallas kernels: 35.1 us -> 34.6 us  [shards(): pl.pallas_call(functools.partial(kernel, dims), out_shape=tuple((pltpu.VM...]
where the time goes in v4:
time: 36.9 us; the launch traced here: 36.7 us
  Pallas kernels  36.1 us (98%)
  between operations  0.64 us (2%)
    pallas_call x1, Pallas kernels, shards(): pl.pallas_call(functools.partial(kernel, dims), out_shape=tuple((pltpu.VM...  34.6 us
    pallas_call x1, Pallas kernels, shards(): pl.pallas_call(write_out, out_shape=shapes, in_specs=[pl.BlockSpec(memory...  1.55 us

profile of v4, /device:TPU:1, one launch (start us, length us, event | category | flops | bytes accessed | tf_op | source)
XLA Modules:
  0.0 36.7 jit_solution(8128429401478362130)
XLA Ops:
  0.6 34.6 %shard_map.84 = (f32[2304,128]{1,0:T(8,128)S(1)}, f32[2304,128]{1,0:T(8,128)S(1)}, f32[384,128]{1,0:T(8,128)S(1)}, f32[8,256]{1,0:T(8,128)S(1)}) custom-call(f32[2304,128]{1,0:T(8,128)} %bitcast.7, f32[2304,128]{1,0:T(8,128)} %bitcast.8, f32[384,128]{1,0:T(8,128)} %bitcast.9, s32[256,128]{1,0:T(8,128)} %lists_hbm.1, s32[256]{0:T(256)} %mask_hbm.1), custom_call_target="tpu_custom_call" | custom-call | tf_op jit(solution)/shard_map/pallas_call | solution.py:665
  35.2 1.5 %shard_map.85 = (f32[2304,128]{1,0:T(8,128)}, f32[2304,128]{1,0:T(8,128)}, f32[384,128]{1,0:T(8,128)}, f32[8,256]{1,0:T(8,128)}) custom-call(f32[2304,128]{1,0:T(8,128)S(1)} %get-tuple-element.12.refs_0_, f32[2304,128]{1,0:T(8,128)S(1)} %get-tuple-element.13.refs_1_, f32[384,128]{1,0:T(8,128)S(1)} %get-tuple-element.14.refs_2_, ...), custom_call_target="tpu_custom_call" | custom-call | tf_op jit(solution)/shard_map/pallas_call | solution.py:705

commit v5 on v4

--- a/solution.py
+++ b/solution.py
@@ -610,6 +610,8 @@
     last_forward()
     last_adjoint()
 
+    for copy in started:
+        copy.wait_send()
     for copy in last_copies:
         copy.wait_recv()
     turned = product(halves(rows_r[...].reshape(n_gy * 8, 128)), (vtab[0], vtab[1]))
@@ -620,9 +622,6 @@
         value = rows[:, :256] + sign * pltpu.roll(rows[:, 256:], 4, 0)
         out = out + tws[d : d + 1, :256] * value + tws[d : d + 1, 256:] * (sign * pltpu.roll(value, 4, 0))
     far_ref[...] = out * (1.0 / math.sqrt(CX * CY))
-
-    for copy in started:
-        copy.wait_send()
 
 
 PIECES = ((0, 4), (1, 4), (2, 1), (3, 1))

time: 36.9 us -> 36.8 us (level)
  no operation moved by 1% of the time
where the time goes in v5:
time: 36.8 us; the launch traced here: 36.7 us
  Pallas kernels  36 us (98%)
  between operations  0.64 us (2%)
    pallas_call x1, Pallas kernels, shards(): pl.pallas_call(functools.partial(kernel, dims), out_shape=tuple((pltpu.VM...  34.5 us
    pallas_call x1, Pallas kernels, shards(): pl.pallas_call(write_out, out_shape=shapes, in_specs=[pl.BlockSpec(memory...  1.55 us

profile of v5, /device:TPU:1, one launch (start us, length us, event | category | flops | bytes accessed | tf_op | source)
XLA Modules:
  0.0 36.7 jit_solution(6012276231984437816)
XLA Ops:
  0.6 34.5 %shard_map.84 = (f32[2304,128]{1,0:T(8,128)S(1)}, f32[2304,128]{1,0:T(8,128)S(1)}, f32[384,128]{1,0:T(8,128)S(1)}, f32[8,256]{1,0:T(8,128)S(1)}) custom-call(f32[2304,128]{1,0:T(8,128)} %bitcast.7, f32[2304,128]{1,0:T(8,128)} %bitcast.8, f32[384,128]{1,0:T(8,128)} %bitcast.9, s32[256,128]{1,0:T(8,128)} %lists_hbm.1, s32[256]{0:T(256)} %mask_hbm.1), custom_call_target="tpu_custom_call" | custom-call | tf_op jit(solution)/shard_map/pallas_call | solution.py:664
  35.1 1.5 %shard_map.85 = (f32[2304,128]{1,0:T(8,128)}, f32[2304,128]{1,0:T(8,128)}, f32[384,128]{1,0:T(8,128)}, f32[8,256]{1,0:T(8,128)}) custom-call(f32[2304,128]{1,0:T(8,128)S(1)} %get-tuple-element.12.refs_0_, f32[2304,128]{1,0:T(8,128)S(1)} %get-tuple-element.13.refs_1_, f32[384,128]{1,0:T(8,128)S(1)} %get-tuple-element.14.refs_2_, ...), custom_call_target="tpu_custom_call" | custom-call | tf_op jit(solution)/shard_map/pallas_call | solution.py:704
